TPU v7x, 256 devices: a whole 4x4x8 slice. The times are simulated.
256 devices in a mesh: seq: 32 (over z, x_lo, core), head: 8 (over x_hi, y).
Axes of the slice: x: 4 (x_hi: 2, x_lo: 2; x = x_hi * 2 + x_lo), y: 4, z: 8, core: 2. Of those that a mesh axis runs over, the one named last changes fastest.
Arguments:
- q_raw: bfloat16 [32768, 4096], P('seq', 'head'), may hold values from -6 to 6
- k_raw: bfloat16 [32768, 2048], P('seq', 'head'), may hold values from -6 to 6
- values: bfloat16 [32768, 2048], P('seq', 'head'), may hold values from -6 to 6
- grad_out: bfloat16 [32768, 4096], P('seq', 'head'), may hold values from -6 to 6
- segment_ids: int32 [32768], replicated, may hold values from 0 to 31, never falling along the last dimension, each value on 1 to 2048 neighbouring positions
- q_gain: float32 [128], replicated, may hold values from 0.5 to 4
- k_gain: float32 [128], replicated, may hold values from 0.5 to 4
Outputs:
- q_grad: bfloat16 [32768, 4096], P('seq', 'head')
- k_grad: bfloat16 [32768, 2048], P('seq', 'head')
- v_grad: bfloat16 [32768, 2048], P('seq', 'head')
- q_gain_grad: float32 [128], replicated
- k_gain_grad: float32 [128], replicated
Inputs may be any that keep to these rules, and one draw needn't show every extreme that they name: `segment_ids`: ids never fall along the tokens; some document holds exactly 2048 tokens.
All inputs are finite; a program needn't handle non-finite values.
Results may differ from a plain program's by a relative error of at most 0.033.
The roundings to bfloat16 on the way count: a program that leaves them out, or rounds other values in their place, can miss the bound.
Values may be sent and summed in bfloat16 or wider, within the bound.
No kernel may reach another device: no remote copies, remote signals or barrier semaphores. Data moves between devices by JAX's collectives and lax.ppermute only.
A program may use at most 128 MiB of HBM per device.

v0:
```python
import jax
import jax.numpy as jnp
from jax import lax
from jax.sharding import PartitionSpec as P

WINDOW = 1024
BLOCK = 512


SCALE = 168.0 ** (-0.5)
EPS = 1e-06
BASE = 10000.0


def shifted(block, axis, distance):
    devices = range(lax.axis_size(axis))
    route = [(i - distance, i) for i in devices if i - distance in devices]
    return lax.ppermute(block, axis, route)


def angles(positions, dim):
    half = dim // 2
    freq = BASE ** (-jnp.arange(half, dtype=jnp.float32) * 2.0 / dim)
    angle = positions.astype(jnp.float32)[:, None] * freq[None, :]
    angle = jnp.concatenate([angle, angle], axis=1)
    return (jnp.cos(angle), jnp.sin(angle))


def rotate(x):
    half = x.shape[-1] // 2
    return jnp.concatenate([-x[..., half:], x[..., :half]], axis=-1)


def rotate_back(z):
    half = z.shape[-1] // 2
    return jnp.concatenate([z[..., half:], -z[..., :half]], axis=-1)


def normed(raw, gain, cosv, sinv, factor):
    x = raw.astype(jnp.float32)
    rstd = lax.rsqrt(jnp.mean(x * x, axis=-1, keepdims=True) + EPS)
    y = x * rstd * gain
    out = (y * cosv[:, None, :] + rotate(y) * sinv[:, None, :]) * factor
    return (out.astype(jnp.bfloat16), rstd)


def norm_back(raw, gain, rstd, grad, cosv, sinv, factor):
    x = raw.astype(jnp.float32)
    g = grad * factor
    dy = g * cosv[:, None, :] + rotate_back(g * sinv[:, None, :])
    gy = dy * gain
    dx = rstd * gy - x * rstd * rstd * rstd * jnp.mean(gy * x, axis=-1, keepdims=True)
    return (dx.astype(jnp.bfloat16), jnp.sum(dy * x * rstd, axis=(0, 1)))


def allowed(qpos, kpos, qseg, kseg):
    gap = qpos[:, None] - kpos[None, :]
    return (qseg[:, None] == kseg[None, :]) & (gap >= 0) & (gap < WINDOW)


def propagate(qb, kb, vb, gb, prob, weights, delta):
    dprob = jnp.einsum("qhgd,khd->hgqk", gb, vb, preferred_element_type=jnp.float32)
    dscore = (prob * (dprob - delta[..., None])).astype(jnp.bfloat16)
    dq = jnp.einsum("hgqk,khd->qhgd", dscore, kb, preferred_element_type=jnp.float32)
    dk = jnp.einsum("hgqk,qhgd->khd", dscore, qb, preferred_element_type=jnp.float32)
    dv = jnp.einsum("hgqk,qhgd->khd", weights, gb, preferred_element_type=jnp.float32)
    return (dq, dk, dv)


def attend(qb, kb, vb, gb, mask):
    scores = jnp.einsum("qhgd,khd->hgqk", qb, kb, preferred_element_type=jnp.float32)
    masked = jnp.where(mask, scores, -jnp.inf)
    top = jnp.max(masked, axis=-1, keepdims=True)
    lse = top + jnp.log(jnp.sum(jnp.exp(masked - top), axis=-1, keepdims=True))
    prob = jnp.where(mask, jnp.exp(scores - lse), 0.0)
    weights = prob.astype(jnp.bfloat16)
    output = jnp.einsum("hgqk,khd->qhgd", weights, vb, preferred_element_type=jnp.float32)
    delta = jnp.transpose(jnp.sum(gb.astype(jnp.float32) * output, axis=-1), (1, 2, 0))
    dq, dk, dv = propagate(qb, kb, vb, gb, prob, weights, delta)
    return (dq, dk, dv, lse[..., 0], delta)


def local(q_raw, k_raw, values, grad_out, segment_ids, q_gain, k_gain):
    tok = q_raw.shape[0]
    dim = q_gain.shape[0]
    q_local = q_raw.shape[1] // dim
    kv_local = k_raw.shape[1] // dim
    group = q_local // kv_local
    start = lax.axis_index("seq") * tok
    positions = start + jnp.arange(tok, dtype=jnp.int32)
    cosv, sinv = angles(positions, dim)
    queries, q_rstd = normed(q_raw.reshape(tok, q_local, dim), q_gain, cosv, sinv, SCALE)
    keys, k_rstd = normed(k_raw.reshape(tok, kv_local, dim), k_gain, cosv, sinv, 1.0)
    vals = values.reshape(tok, kv_local, dim)
    grads = grad_out.reshape(tok, kv_local, group, dim)
    qgroups = queries.reshape(tok, kv_local, group, dim)
    prev_keys, prev_vals = shifted((keys, vals), "seq", 1)
    all_keys = jnp.concatenate([prev_keys, keys], axis=0)
    all_vals = jnp.concatenate([prev_vals, vals], axis=0)
    padded_seg = jnp.concatenate(
        [jnp.full((tok,), -1, jnp.int32), segment_ids, jnp.full((tok,), -2, jnp.int32)]
    )
    q_seg = lax.dynamic_slice_in_dim(padded_seg, start + tok, tok)
    k_seg = lax.dynamic_slice_in_dim(padded_seg, start, 2 * tok)
    k_pos = start - tok + jnp.arange(2 * tok, dtype=jnp.int32)
    span = WINDOW + BLOCK

    def step(carry, index):
        dk_acc, dv_acc = carry
        first = index * BLOCK
        kfirst = first + tok - WINDOW
        qb = lax.dynamic_slice_in_dim(qgroups, first, BLOCK)
        gb = lax.dynamic_slice_in_dim(grads, first, BLOCK)
        kb = lax.dynamic_slice_in_dim(all_keys, kfirst, span)
        vb = lax.dynamic_slice_in_dim(all_vals, kfirst, span)
        mask = allowed(
            lax.dynamic_slice_in_dim(positions, first, BLOCK),
            lax.dynamic_slice_in_dim(k_pos, kfirst, span),
            lax.dynamic_slice_in_dim(q_seg, first, BLOCK),
            lax.dynamic_slice_in_dim(k_seg, kfirst, span),
        )
        dq, dk, dv, lse, delta = attend(qb, kb, vb, gb, mask)
        dk_acc = lax.dynamic_update_slice_in_dim(
            dk_acc, lax.dynamic_slice_in_dim(dk_acc, kfirst, span) + dk, kfirst, 0
        )
        dv_acc = lax.dynamic_update_slice_in_dim(
            dv_acc, lax.dynamic_slice_in_dim(dv_acc, kfirst, span) + dv, kfirst, 0
        )
        return ((dk_acc, dv_acc), (dq, lse, delta))

    zeros = jnp.zeros((2 * tok, kv_local, dim), jnp.float32)
    (dk_acc, dv_acc), (dq_blocks, lse_all, delta_all) = lax.scan(
        step, (zeros, zeros), jnp.arange(tok // BLOCK, dtype=jnp.int32)
    )
    dk_back, dv_back = (
        shifted(dk_acc[:tok].astype(jnp.bfloat16), "seq", -1).astype(jnp.float32),
        shifted(dv_acc[:tok].astype(jnp.bfloat16), "seq", -1).astype(jnp.float32),
    )
    dk_own = dk_acc[tok:] + dk_back
    dv_own = dv_acc[tok:] + dv_back
    dq_all = dq_blocks.reshape(tok, q_local, dim)
    q_grad, q_part = norm_back(
        q_raw.reshape(tok, q_local, dim), q_gain, q_rstd, dq_all, cosv, sinv, SCALE
    )
    k_grad, k_part = norm_back(
        k_raw.reshape(tok, kv_local, dim), k_gain, k_rstd, dk_own, cosv, sinv, 1.0
    )
    q_gain_grad, k_gain_grad = lax.psum((q_part, k_part), ("seq", "head"))
    v_grad = dv_own.astype(jnp.bfloat16)
    return (
        q_grad.reshape(tok, q_local * dim),
        k_grad.reshape(tok, kv_local * dim),
        v_grad.reshape(tok, kv_local * dim),
        q_gain_grad,
        k_gain_grad,
    )


def solution(mesh):
    in_specs = (
        P("seq", "head"),
        P("seq", "head"),
        P("seq", "head"),
        P("seq", "head"),
        P(),
        P(),
        P(),
    )
    out_specs = (P("seq", "head"), P("seq", "head"), P("seq", "head"), P(), P())
    return jax.shard_map(local, mesh=mesh, in_specs=in_specs, out_specs=out_specs, check_vma=False)
```

profile of v0, /device:TPU:14, one launch (start us, length us, event | category | flops | bytes accessed | tf_op | source)
XLA Modules:
  0.0 263.9 jit_solution(988067718874674543)
XLA Ops:
  0.7 1.2 copy.79
  2.3 1.1 slice_negate_fusion.3
  3.6 2.9 %broadcast_multiply_fusion.2 = (f32[1024,128]{1,0:T(8,128)}, f32[1024,128]{1,0:T(8,128)}, f32[1024,128]{1,0:T(8,128)S(1)}, f32[1024,128]{1,0:T(8,128)S(1)}) fusion(f32[1024,64]{1,0:T(8,128)S(1)} %broadcast_multiply_fusion.3), kind=kLoop, calls=%fused_computation.92 | loop fusion | flops 393216 | bytes 2359296 | tf_op jit(solution)/shard_map/mul | solution.py:50
  6.9 2.7 %fusion.43 = bf16[1024,2,128]{0,2,1:T(8,128)(2,1)} fusion(f32[1024,2,64]{0,2,1:T(8,128)} %get-tuple-element.355, f32[1024,2,64]{0,2,1:T(8,128)} %get-tuple-element.354, f32[1024,128]{0,1:T(8,128)S(1)} %copy.81, f32[1024,128]{0,1:T(8,128)S(1)} %copy.80, f32[128]{0:T(128)S(1)} %copy-done.32, f32[1024,2]{0,1:T(2,128)S(1)} %add_rsqrt_fusion.1, ...), kind=kLoop, calls=%fused_computation.71 | loop fusion | flops 1835008 | bytes 3678720 | tf_op jit(solution)/shard_map/convert_element_type | solution.py:44
  9.6 1.9 collective-permute-start
  11.5 2.1 copy.82
  13.6 4.2 %collective-permute-start.1 = (bf16[1024,2,128]{0,2,1:T(8,128)(2,1)}, bf16[1024,2,128]{0,2,1:T(8,128)(2,1)}, u32[]{:S(2)}, u32[]{:S(2)}) collective-permute-start(bf16[1024,2,128]{0,2,1:T(8,128)(2,1)} %bitcast.25), channel_id=1, source_target_pairs={{0,8},{8,16},{16,24},{24,32},{32,40},{40,48},{48,56},{56,64},{64,7... | collective-permute-start | bytes 1572872 | tf_op jit(solution)/shard_map/ppermute | solution.py:18
  17.8 1.5 copy.75
  20.4 1.5 slice_negate_fusion.1
  21.9 3.1 %copy.77 = f32[1024,4,64]{2,0,1:T(8,128)} copy(f32[1024,4,64]{0,2,1:T(8,128)} %get-tuple-element.350) | data formatting | bytes 2097152 | tf_op jit(solution)/shard_map/neg | solution.py:31
  25.0 3.2 %copy.78 = f32[1024,4,64]{2,0,1:T(8,128)} copy(f32[1024,4,64]{0,2,1:T(8,128)} %get-tuple-element.351) | data formatting | bytes 2097152 | tf_op jit(solution)/shard_map/slice | solution.py:31
  28.2 1.8 copy.76
  30.2 4.5 %fusion.40 = bf16[1024,2,2,128]{3,0,2,1:T(8,128)(2,1)} fusion(f32[1024,2,2,64]{3,0,2,1:T(8,128)} %bitcast.201, f32[1024,2,2,64]{3,0,2,1:T(8,128)} %bitcast.200, f32[1024,2,2,128]{3,0,2,1:T(8,128)} %copy.76, f32[1024,128]{1,0:T(8,128)} %copy-done.12, f32[1024,128]{1,0:T(8,128)} %copy-done.13, f32[128]{0:T(128)S(1)} %copy-done.30, f32[1024,2,2]{0,2,1:T(2,128)S(1)} %rsqrt.25), kind=kLoop, calls=%fused_computation.56 | loop fusion | flops 4194304 | bytes 6308352 | tf_op jit(solution)/shard_map/convert_element_type | solution.py:44
  34.8 7.5 %fusion.45 = f32[2,512,128]{1,0,2:T(2,128)} fusion(f32[2,512,64]{1,0,2:T(2,128)S(1)} %broadcast_multiply_fusion.4), kind=kLoop, calls=%fused_computation.88 | loop fusion | flops 262144 | bytes 786432 | tf_op jit(solution)/shard_map/mul | solution.py:50
  42.2 0.6 rsqrt.27
  42.9 3.1 %reshape.208 = f32[2,512,2,2,128]{1,0,4,3,2:T(2,128)} reshape(bf16[1024,512]{0,1:T(8,128)(2,1)S(1)} %copy.75) | data formatting | bytes 3145728 | tf_op jit(solution)/shard_map/convert_element_type | solution.py:40
  45.9 1.3 copy.83
  47.2 1.0 copy.88
  48.8 1.3 pad_maximum_fusion.1
  50.1 2.3 pad_maximum_fusion.2
  52.5 1.6 broadcast_in_dim.77
  54.0 1.5 broadcast_in_dim.77.clone
  55.6 84.9 %while.18 = (s32[]{:T(128)}, f32[2048,2,128]{0,2,1:T(8,128)}, f32[2048,2,128]{0,2,1:T(8,128)}, f32[2,512,2,2,128]{1,4,3,2,0:T(8,128)}, s32[2]{0:T(128)S(1)}, /*i...) while((s32[]{:T(128)}, f32[2048,2,128]{0,2,1:T(8,128)}, ...), condition=%wide.region_6.7_spmd, body=%wide.region_2.6_spmd.sunk | while | flops 4888457216 | bytes 236069792 | solution.py:132
  57.1 1.3 fusion.82
  58.4 3.2 %fusion.83 = (f32[2,2,512]{2,1,0:T(2,128)S(1)}, f32[2,1536,512,2]{2,1,3,0:T(8,128)S(1)}) fusion(pred[512,1536]{0,1:T(8,128)(4,1)S(1)} %fusion.82, bf16[1024,2,2,128]{3,0,2,1:T(8,128)(2,1)} %get-tuple-element.484, s32[]{:T(128)S(6)} %select_n.80, bf16[2048,2,128]{0,2,1:T(8,128)(2,1)S(1)} %get-tuple-element.489, s32[]{:T(128)S(6)} %select_n.79), kind=kOutput, calls=%fused_computation.8.clone.1 | convolution fusion | flops 811595776 | bytes 14688264 | tf_op jit(solution)/shard_map/while/body/eval_jaxpr/qhgd,khd->hgqk/dot_general | solution.py:71
  61.7 2.3 exponential_reduce_fusion.2
  63.9 2.4 constant_dynamic-slice_fusion.2
  66.4 4.9 %fusion.87 = f32[2048,2,128]{0,2,1:T(8,128)} fusion(f32[2048,2,128]{0,2,1:T(8,128)} %get-tuple-element.463, s32[]{:T(128)S(6)} %select_n.79, bf16[512,2,2,128]{0,3,2,1:T(8,128)(2,1)} %constant_dynamic-slice_fusion.2, f32[2,1536,512,2]{2,1,3,0:T(8,128)S(1)} %get-tuple-element.441, f32[2,2,512]{2,1,0:T(2,128)S(1)} %log_add_fusion.2, ...), kind=kOutput, calls=%fused_computation.19.clone.1 | convolution fusion | flops 815136768 | bytes 17047556 | tf_op jit(solution)/shard_map/while/body/eval_jaxpr/hgqk,qhgd->khd/dot_general | solution.py:66
  71.3 1.3 copy.126
  72.6 8.7 %fusion.84 = f32[512,2,2]{0,2,1:T(2,128)S(1)} fusion(bf16[512,2,2,128]{3,0,2,1:T(8,128)(2,1)S(1)} %copy.126, bf16[2048,2,128]{0,2,1:T(8,128)(2,1)} %get-tuple-element.490, s32[]{:T(128)S(6)} %select_n.79, f32[2,1536,512,2]{2,1,3,0:T(8,128)} %copy-done, f32[2,2,512]{2,1,0:T(2,128)S(1)} %log_add_fusion.2, pred[512,1536]{0,1:T(8,128)(4,1)S(1)} %fusion.82), kind=kOutput, calls=%fused_computation.24.clone.1 | convolution fusion | flops 815527936 | bytes 14696452 | tf_op jit(solution)/shard_map/while/body/eval_jaxpr/hgqk,khd->qhgd/dot_general | solution.py:77
  81.4 7.0 %fusion.85 = bf16[2,2,512,1536]{2,3,1,0:T(8,128)(2,1)} fusion(f32[2,1536,512,2]{2,1,3,0:T(8,128)S(1)} %copy-done.1, bf16[512,2,2,128]{0,3,2,1:T(8,128)(2,1)} %constant_dynamic-slice_fusion.2, f32[2,2,512]{2,1,0:T(2,128)S(1)} %bitcast.206, f32[2,2,512]{2,1,0:T(2,128)S(1)} %log_add_fusion.2, pred[512,1536]{0,1:T(8,128)(4,1)S(1)} %fusion.82, ...), kind=kOutput, calls=%fused_computation.2.clone.1 | convolution fusion | flops 821035008 | bytes 20987908 | tf_op jit(solution)/shard_map/while/body/eval_jaxpr/qhgd,khd->hgqk/dot_general | solution.py:62
  88.4 4.9 %fusion.88 = f32[2,512,2,2,128]{1,4,3,2,0:T(8,128)} fusion(f32[2,512,2,2,128]{1,4,3,2,0:T(8,128)} %get-tuple-element.464, s32[]{:T(128)} %get-tuple-element.461, bf16[2,2,512,1536]{2,3,1,0:T(8,128)(2,1)} %fusion.85, bf16[2048,2,128]{0,2,1:T(8,128)(2,1)S(1)} %get-tuple-element.489, s32[]{:T(128)S(6)} %select_n.79), kind=kOutput, calls=%fused_computation.21.clone.1 | convolution fusion | flops 805306368 | bytes 8126980 | tf_op jit(solution)/shard_map/while/body/eval_jaxpr/hgqk,khd->qhgd/dot_general | solution.py:64
  93.3 4.8 %fusion.86 = f32[2048,2,128]{0,2,1:T(8,128)} fusion(f32[2048,2,128]{0,2,1:T(8,128)} %get-tuple-element.462, s32[]{:T(128)S(6)} %select_n.79, bf16[2,2,512,1536]{2,3,1,0:T(8,128)(2,1)S(1)} %copy-done.2, bf16[1024,2,2,128]{3,0,2,1:T(8,128)(2,1)S(1)} %copy-done.5, s32[]{:T(128)S(6)} %select_n.80), kind=kOutput, calls=%fused_computation.17.clone.1 | convolution fusion | flops 805699584 | bytes 9961480 | tf_op jit(solution)/shard_map/while/body/eval_jaxpr/hgqk,qhgd->khd/dot_general | solution.py:65
  99.6 1.3 fusion.82
  100.9 3.2 %fusion.83 = (f32[2,2,512]{2,1,0:T(2,128)S(1)}, f32[2,1536,512,2]{2,1,3,0:T(8,128)S(1)}) fusion(pred[512,1536]{0,1:T(8,128)(4,1)S(1)} %fusion.82, bf16[1024,2,2,128]{3,0,2,1:T(8,128)(2,1)} %get-tuple-element.484, s32[]{:T(128)S(6)} %select_n.80, bf16[2048,2,128]{0,2,1:T(8,128)(2,1)S(1)} %get-tuple-element.489, s32[]{:T(128)S(6)} %select_n.79), kind=kOutput, calls=%fused_computation.8.clone.1 | convolution fusion | flops 811595776 | bytes 14688264 | tf_op jit(solution)/shard_map/while/body/eval_jaxpr/qhgd,khd->hgqk/dot_general | solution.py:71
  104.1 2.3 exponential_reduce_fusion.2
  106.4 2.4 constant_dynamic-slice_fusion.2
  108.8 4.9 %fusion.87 = f32[2048,2,128]{0,2,1:T(8,128)} fusion(f32[2048,2,128]{0,2,1:T(8,128)} %get-tuple-element.463, s32[]{:T(128)S(6)} %select_n.79, bf16[512,2,2,128]{0,3,2,1:T(8,128)(2,1)} %constant_dynamic-slice_fusion.2, f32[2,1536,512,2]{2,1,3,0:T(8,128)S(1)} %get-tuple-element.441, f32[2,2,512]{2,1,0:T(2,128)S(1)} %log_add_fusion.2, ...), kind=kOutput, calls=%fused_computation.19.clone.1 | convolution fusion | flops 815136768 | bytes 17047556 | tf_op jit(solution)/shard_map/while/body/eval_jaxpr/hgqk,qhgd->khd/dot_general | solution.py:66
  113.8 1.3 copy.126
  115.1 8.7 %fusion.84 = f32[512,2,2]{0,2,1:T(2,128)S(1)} fusion(bf16[512,2,2,128]{3,0,2,1:T(8,128)(2,1)S(1)} %copy.126, bf16[2048,2,128]{0,2,1:T(8,128)(2,1)} %get-tuple-element.490, s32[]{:T(128)S(6)} %select_n.79, f32[2,1536,512,2]{2,1,3,0:T(8,128)} %copy-done, f32[2,2,512]{2,1,0:T(2,128)S(1)} %log_add_fusion.2, pred[512,1536]{0,1:T(8,128)(4,1)S(1)} %fusion.82), kind=kOutput, calls=%fused_computation.24.clone.1 | convolution fusion | flops 815527936 | bytes 14696452 | tf_op jit(solution)/shard_map/while/body/eval_jaxpr/hgqk,khd->qhgd/dot_general | solution.py:77
  123.8 7.0 %fusion.85 = bf16[2,2,512,1536]{2,3,1,0:T(8,128)(2,1)} fusion(f32[2,1536,512,2]{2,1,3,0:T(8,128)S(1)} %copy-done.1, bf16[512,2,2,128]{0,3,2,1:T(8,128)(2,1)} %constant_dynamic-slice_fusion.2, f32[2,2,512]{2,1,0:T(2,128)S(1)} %bitcast.206, f32[2,2,512]{2,1,0:T(2,128)S(1)} %log_add_fusion.2, pred[512,1536]{0,1:T(8,128)(4,1)S(1)} %fusion.82, ...), kind=kOutput, calls=%fused_computation.2.clone.1 | convolution fusion | flops 821035008 | bytes 20987908 | tf_op jit(solution)/shard_map/while/body/eval_jaxpr/qhgd,khd->hgqk/dot_general | solution.py:62
  130.8 4.9 %fusion.88 = f32[2,512,2,2,128]{1,4,3,2,0:T(8,128)} fusion(f32[2,512,2,2,128]{1,4,3,2,0:T(8,128)} %get-tuple-element.464, s32[]{:T(128)} %get-tuple-element.461, bf16[2,2,512,1536]{2,3,1,0:T(8,128)(2,1)} %fusion.85, bf16[2048,2,128]{0,2,1:T(8,128)(2,1)S(1)} %get-tuple-element.489, s32[]{:T(128)S(6)} %select_n.79), kind=kOutput, calls=%fused_computation.21.clone.1 | convolution fusion | flops 805306368 | bytes 8126980 | tf_op jit(solution)/shard_map/while/body/eval_jaxpr/hgqk,khd->qhgd/dot_general | solution.py:64
  135.7 4.7 %fusion.86 = f32[2048,2,128]{0,2,1:T(8,128)} fusion(f32[2048,2,128]{0,2,1:T(8,128)} %get-tuple-element.462, s32[]{:T(128)S(6)} %select_n.79, bf16[2,2,512,1536]{2,3,1,0:T(8,128)(2,1)S(1)} %copy-done.2, bf16[1024,2,2,128]{3,0,2,1:T(8,128)(2,1)S(1)} %copy-done.5, s32[]{:T(128)S(6)} %select_n.80), kind=kOutput, calls=%fused_computation.17.clone.1 | convolution fusion | flops 805699584 | bytes 9961480 | tf_op jit(solution)/shard_map/while/body/eval_jaxpr/hgqk,qhgd->khd/dot_general | solution.py:65
  140.4 2.1 slice.73
  142.5 1.9 collective-permute-start.2
  144.5 2.0 copy.89
  146.6 2.0 fusion.49
  148.6 0.9 copy.114
  149.5 2.7 %copy.115 = f32[2,512,2,2,64]{1,0,4,3,2:T(2,128)} copy(f32[2,512,2,2,64]{4,1,0,3,2:T(8,128)} %bitcast.194) | data formatting | bytes 2097152 | tf_op jit(solution)/shard_map/concatenate | solution.py:36
  152.2 2.1 slice.72
  154.3 2.8 %collective-permute-start.3 = (bf16[1024,2,128]{0,2,1:T(8,128)(2,1)}, bf16[1024,2,128]{0,2,1:T(8,128)(2,1)}, u32[]{:S(2)}, u32[]{:S(2)}) collective-permute-start(bf16[1024,2,128]{0,2,1:T(8,128)(2,1)} %slice.72), channel_id=1, source_target_pairs={{8,0},{16,8},{24,16},{32,24},{40,32},{48,40},{56,48},{64,56},{72,6... | collective-permute-start | bytes 1572872 | tf_op jit(solution)/shard_map/ppermute | solution.py:18
  157.1 4.8 %maximum_add_fusion = (f32[2,512,2,2,128]{1,0,4,3,2:T(2,128)S(1)}, f32[2,512,2,2,128]{1,0,4,3,2:T(2,128)S(1)}) fusion(f32[2,512,2,2,64]{1,0,4,3,2:T(2,128)} %copy.115, f32[2,512,2,2,64]{1,0,4,3,2:T(2,128)S(1)} %copy.114, f32[2,512,128]{1,0,2:T(2,128)} %fusion.45, f32[2,512,2,2,128]{1,4,3,2,0:T(8,128)} %get-tuple-element.262), kind=kLoop, calls=%fused_computation.58 | loop fusion | flops 1572864 | bytes 8912896 | tf_op jit(solution)/shard_map/add | solution.py:50
  161.9 3.0 %multiply_reduce_fusion = (f32[128]{0:T(128)S(1)}, f32[2,512,2,2]{1,0,3,2:T(2,128)S(1)}) fusion(f32[2,512,2,2,128]{1,0,4,3,2:T(2,128)S(1)} %get-tuple-element.346, f32[2,512,2,2,128]{1,0,4,3,2:T(2,128)S(1)} %copy-done.9, f32[2,512,2,2]{1,0,3,2:T(2,128)S(1)} %copy-done.28, f32[128]{0:T(128)S(1)} %copy-done.31), kind=kLoop, calls=%fused_computation.62 | loop fusion | flops 3141504 | bytes 4228096 | tf_op jit(solution)/shard_map/reduce_sum | solution.py:53
  164.9 1.8 copy.121
  166.8 2.1 pad_maximum_fusion
  168.9 3.0 %copy.90 = f32[1024,4,128]{0,2,1:T(8,128)} copy(f32[1024,4,128]{2,0,1:T(8,128)} %pad_maximum_fusion) | data formatting | bytes 4194304 | tf_op jit(solution)/shard_map/concatenate | solution.py:36
  172.0 3.4 %fusion.36 = bf16[1024,512]{0,1:T(8,128)(2,1)} fusion(f32[1024,4,128]{0,2,1:T(8,128)} %copy.90, f32[1024,512]{0,1:T(8,128)S(1)} %bitcast.198, f32[1024,4]{0,1:T(4,128)S(1)} %bitcast.204, f32[512]{0:T(512)S(1)} %copy-done.29, f32[1024,128]{0,1:T(8,128)} %copy.88, f32[1024,4]{0,1:T(4,128)S(1)} %copy-done.23, bf16[1024,512]{0,1:T(8,128)(2,1)S(1)} %copy-done.8), kind=kLoop, calls=%fused_computation.50 | loop fusion | flops 5767168 | bytes 6850560 | tf_op jit(solution)/shard_map/convert_element_type | solution.py:53
  175.3 2.3 copy.96
  177.7 1.7 fusion.44
  179.7 1.3 add_convert_fusion
  181.1 1.0 copy.117
  182.1 1.9 multiply_reduce_fusion.3
  184.3 1.0 copy.116
  185.3 78.6 %all-reduce = (f32[128]{0:T(128)}, f32[128]{0:T(128)}) all-reduce(f32[128]{0:T(128)S(1)} %get-tuple-element.309, f32[128]{0:T(128)S(1)} %get-tuple-element.311), channel_id=1, replica_groups=mesh['seq'=32,'head'=8] {'seq','head'}, use_global_device_ids=true, to_apply=%region_10.11 | all-reduce | flops 256 | bytes 2048 | tf_op jit(solution)/shard_map/psum | solution.py:148
  (125 shorter events, 5.6 us)
Async XLA Ops:
  0.6 1.4 copy-start.32
  1.9 5.0 %copy-start.3 = (f32[1024,256]{0,1:T(8,128)}, f32[1024,256]{0,1:T(8,128)S(1)}, u32[]{:S(2)}) copy-start(f32[1024,256]{0,1:T(8,128)S(1)} %copy.79) | copy-start | bytes 3145732
  2.1 4.9 %copy-start.25 = (f32[1024,2]{0,1:T(2,128)}, f32[1024,2]{0,1:T(2,128)S(1)}, u32[]{:S(2)}) copy-start(f32[1024,2]{0,1:T(2,128)S(1)} %add_rsqrt_fusion.1) | copy-start | bytes 24580
  6.5 3.1 %copy-start.12 = (f32[1024,128]{1,0:T(8,128)}, f32[1024,128]{1,0:T(8,128)S(1)}, u32[]{:S(2)}) copy-start(f32[1024,128]{1,0:T(8,128)S(1)} %get-tuple-element.358) | copy-start | bytes 1572868
  6.5 3.1 %copy-start.13 = (f32[1024,128]{1,0:T(8,128)}, f32[1024,128]{1,0:T(8,128)S(1)}, u32[]{:S(2)}) copy-start(f32[1024,128]{1,0:T(8,128)S(1)} %get-tuple-element.359) | copy-start | bytes 1572868
  6.7 2.9 %copy-start.16 = (f32[1024,128]{0,1:T(8,128)}, f32[1024,128]{0,1:T(8,128)S(1)}, u32[]{:S(2)}) copy-start(f32[1024,128]{0,1:T(8,128)S(1)} %copy.80) | copy-start | bytes 1572868
  6.9 6.7 %copy-start.14 = (f32[1024,128]{0,1:T(8,128)}, f32[1024,128]{0,1:T(8,128)S(1)}, u32[]{:S(2)}) copy-start(f32[1024,128]{0,1:T(8,128)S(1)} %copy.81) | copy-start | bytes 1572868
  9.6 39.2 %collective-permute-start = (bf16[1024,2,128]{0,2,1:T(8,128)(2,1)}, bf16[1024,2,128]{0,2,1:T(8,128)(2,1)}, u32[]{:S(2)}, u32[]{:S(2)}) collective-permute-start(bf16[1024,2,128]{0,2,1:T(8,128)(2,1)} %fusion.43), channel_id=1, source_target_pairs={{0,8},{8,16},{16,24},{24,32},{32,40},{40,48},{48,56},{56,64},{64,7... | collective-permute-start | bytes 1572872 | tf_op jit(solution)/shard_map/ppermute | solution.py:18
  13.6 36.5 %collective-permute-start.1 = (bf16[1024,2,128]{0,2,1:T(8,128)(2,1)}, bf16[1024,2,128]{0,2,1:T(8,128)(2,1)}, u32[]{:S(2)}, u32[]{:S(2)}) collective-permute-start(bf16[1024,2,128]{0,2,1:T(8,128)(2,1)} %bitcast.25), channel_id=1, source_target_pairs={{0,8},{8,16},{16,24},{24,32},{32,40},{40,48},{48,56},{56,64},{64,7... | collective-permute-start | bytes 1572872 | tf_op jit(solution)/shard_map/ppermute | solution.py:18
  19.3 23.6 %copy-start.7 = (bf16[1024,512]{0,1:T(8,128)(2,1)}, bf16[1024,512]{0,1:T(8,128)(2,1)S(1)}, u32[]{:S(2)}) copy-start(bf16[1024,512]{0,1:T(8,128)(2,1)S(1)} %copy.75) | copy-start | bytes 3145732
  19.3 0.7 copy-start.30
  19.6 22.6 %copy-start.22 = (f32[1024,4]{0,1:T(4,128)}, f32[1024,4]{0,1:T(4,128)S(1)}, u32[]{:S(2)}) copy-start(f32[1024,4]{0,1:T(4,128)S(1)} %add_rsqrt_fusion) | copy-start | bytes 49156
  28.2 2.0 copy-start.27
  30.2 17.0 %copy-start.24 = (s32[34816]{0:T(1024)}, s32[34816]{0:T(1024)S(1)}, u32[]{:S(2)}) copy-start(s32[34816]{0:T(1024)S(1)} %pad_add_fusion) | copy-start | bytes 417796
  34.7 11.2 %copy-start.20 = (bf16[1024,512]{1,0:T(8,128)(2,1)S(1)}, bf16[1024,512]{1,0:T(8,128)(2,1)}, u32[]{:S(2)}) copy-start(bf16[1024,512]{1,0:T(8,128)(2,1)} %param.12) | copy-start | bytes 3145732
  42.9 4.4 %copy-start.19 = (f32[1024,128]{1,0:T(8,128)S(1)}, f32[1024,128]{1,0:T(8,128)}, u32[]{:S(2)}) copy-start(f32[1024,128]{1,0:T(8,128)} %get-tuple-element.356) | copy-start | bytes 1572868
  52.5 3.1 %dynamic-slice-start = ((s32[34816]{0:T(1024)}, s32[]{:T(128)}), s32[2048]{0:T(1024)S(1)}, s32[]{:S(2)}) async-start(s32[34816]{0:T(1024)} %copy-done.24, s32[]{:T(128)} %select_n.54), calls=%async_computation | async-start | bytes 16896 | tf_op jit(solution)/shard_map/dynamic_slice | solution.py:104
  61.7 4.7 %copy-start = (f32[2,1536,512,2]{2,1,3,0:T(8,128)}, f32[2,1536,512,2]{2,1,3,0:T(8,128)S(1)}, u32[]{:S(2)}) copy-start(f32[2,1536,512,2]{2,1,3,0:T(8,128)S(1)} %get-tuple-element.441) | copy-start | bytes 37748740 | tf_op jit(solution)/shard_map/while
  72.6 8.7 %copy-start.1 = (f32[2,1536,512,2]{2,1,3,0:T(8,128)S(1)}, f32[2,1536,512,2]{2,1,3,0:T(8,128)}, u32[]{:S(2)}) copy-start(f32[2,1536,512,2]{2,1,3,0:T(8,128)} %copy-done) | copy-start | bytes 37748740 | tf_op jit(solution)/shard_map/while
  72.6 8.7 %copy-start.21 = (bf16[2048,2,128]{0,2,1:T(8,128)(2,1)S(1)}, bf16[2048,2,128]{0,2,1:T(8,128)(2,1)}, u32[]{:S(2)}) copy-start(bf16[2048,2,128]{0,2,1:T(8,128)(2,1)} %get-tuple-element.490) | copy-start | bytes 3145732 | tf_op jit(solution)/shard_map/while
  88.4 4.9 %copy-start.2 = (bf16[2,2,512,1536]{2,3,1,0:T(8,128)(2,1)S(1)}, bf16[2,2,512,1536]{2,3,1,0:T(8,128)(2,1)}, u32[]{:S(2)}) copy-start(bf16[2,2,512,1536]{2,3,1,0:T(8,128)(2,1)} %fusion.85) | copy-start | bytes 18874372 | tf_op jit(solution)/shard_map/while
  88.4 4.9 %copy-start.5 = (bf16[1024,2,2,128]{3,0,2,1:T(8,128)(2,1)S(1)}, bf16[1024,2,2,128]{3,0,2,1:T(8,128)(2,1)}, u32[]{:S(2)}) copy-start(bf16[1024,2,2,128]{3,0,2,1:T(8,128)(2,1)} %get-tuple-element.484) | copy-start | bytes 3145732 | tf_op jit(solution)/shard_map/while
  104.1 4.7 %copy-start = (f32[2,1536,512,2]{2,1,3,0:T(8,128)}, f32[2,1536,512,2]{2,1,3,0:T(8,128)S(1)}, u32[]{:S(2)}) copy-start(f32[2,1536,512,2]{2,1,3,0:T(8,128)S(1)} %get-tuple-element.441) | copy-start | bytes 37748740 | tf_op jit(solution)/shard_map/while
  115.1 8.7 %copy-start.1 = (f32[2,1536,512,2]{2,1,3,0:T(8,128)S(1)}, f32[2,1536,512,2]{2,1,3,0:T(8,128)}, u32[]{:S(2)}) copy-start(f32[2,1536,512,2]{2,1,3,0:T(8,128)} %copy-done) | copy-start | bytes 37748740 | tf_op jit(solution)/shard_map/while
  115.1 8.7 %copy-start.21 = (bf16[2048,2,128]{0,2,1:T(8,128)(2,1)S(1)}, bf16[2048,2,128]{0,2,1:T(8,128)(2,1)}, u32[]{:S(2)}) copy-start(bf16[2048,2,128]{0,2,1:T(8,128)(2,1)} %get-tuple-element.490) | copy-start | bytes 3145732 | tf_op jit(solution)/shard_map/while
  130.8 4.9 %copy-start.2 = (bf16[2,2,512,1536]{2,3,1,0:T(8,128)(2,1)S(1)}, bf16[2,2,512,1536]{2,3,1,0:T(8,128)(2,1)}, u32[]{:S(2)}) copy-start(bf16[2,2,512,1536]{2,3,1,0:T(8,128)(2,1)} %fusion.85) | copy-start | bytes 18874372 | tf_op jit(solution)/shard_map/while
  130.8 4.9 %copy-start.5 = (bf16[1024,2,2,128]{3,0,2,1:T(8,128)(2,1)S(1)}, bf16[1024,2,2,128]{3,0,2,1:T(8,128)(2,1)}, u32[]{:S(2)}) copy-start(bf16[1024,2,2,128]{3,0,2,1:T(8,128)(2,1)} %get-tuple-element.484) | copy-start | bytes 3145732 | tf_op jit(solution)/shard_map/while
  142.5 35.1 %collective-permute-start.2 = (bf16[1024,2,128]{0,2,1:T(8,128)(2,1)}, bf16[1024,2,128]{0,2,1:T(8,128)(2,1)}, u32[]{:S(2)}, u32[]{:S(2)}) collective-permute-start(bf16[1024,2,128]{0,2,1:T(8,128)(2,1)} %slice.73), channel_id=1, source_target_pairs={{8,0},{16,8},{24,16},{32,24},{40,32},{48,40},{56,48},{64,56},{72,6... | collective-permute-start | bytes 1572872 | tf_op jit(solution)/shard_map/ppermute | solution.py:18
  144.5 2.0 copy-start.18
  154.3 7.6 %copy-start.9 = (f32[2,512,2,2,128]{1,0,4,3,2:T(2,128)S(1)}, f32[2,512,2,2,128]{1,0,4,3,2:T(2,128)}, u32[]{:S(2)}) copy-start(f32[2,512,2,2,128]{1,0,4,3,2:T(2,128)} %reshape.208) | copy-start | bytes 6291460
  154.3 7.6 %copy-start.28 = (f32[2,512,2,2]{1,0,3,2:T(2,128)S(1)}, f32[2,512,2,2]{1,0,3,2:T(2,128)}, u32[]{:S(2)}) copy-start(f32[2,512,2,2]{1,0,3,2:T(2,128)} %rsqrt.27) | copy-start | bytes 49156
  154.3 7.6 %copy-start.31 = (f32[128]{0:T(128)S(1)}, f32[128]{0:T(128)}, u32[]{:S(2)}) copy-start(f32[128]{0:T(128)} %param.14) | copy-start | bytes 1540
  154.3 25.2 %collective-permute-start.3 = (bf16[1024,2,128]{0,2,1:T(8,128)(2,1)}, bf16[1024,2,128]{0,2,1:T(8,128)(2,1)}, u32[]{:S(2)}, u32[]{:S(2)}) collective-permute-start(bf16[1024,2,128]{0,2,1:T(8,128)(2,1)} %slice.72), channel_id=1, source_target_pairs={{8,0},{16,8},{24,16},{32,24},{40,32},{48,40},{56,48},{64,56},{72,6... | collective-permute-start | bytes 1572872 | tf_op jit(solution)/shard_map/ppermute | solution.py:18
  164.9 1.9 copy-start.6
  168.9 3.1 %copy-start.8 = (bf16[1024,512]{0,1:T(8,128)(2,1)S(1)}, bf16[1024,512]{0,1:T(8,128)(2,1)}, u32[]{:S(2)}) copy-start(bf16[1024,512]{0,1:T(8,128)(2,1)} %copy-done.7) | copy-start | bytes 3145732
  168.9 3.1 %copy-start.10 = (f32[64,8,2,512]{3,1,2,0:T(8,128)S(1)}, f32[64,8,2,512]{3,1,2,0:T(8,128)}, u32[]{:S(2)}) copy-start(f32[64,8,2,512]{3,1,2,0:T(8,128)} %copy.121) | copy-start | bytes 6291460
  168.9 3.1 %copy-start.23 = (f32[1024,4]{0,1:T(4,128)S(1)}, f32[1024,4]{0,1:T(4,128)}, u32[]{:S(2)}) copy-start(f32[1024,4]{0,1:T(4,128)} %copy-done.22) | copy-start | bytes 49156
  168.9 3.1 %copy-start.29 = (f32[512]{0:T(512)S(1)}, f32[512]{0:T(512)}, u32[]{:S(2)}) copy-start(f32[512]{0:T(512)} %broadcast_bitcast_fusion) | copy-start | bytes 6148
  175.3 2.3 copy-start.15
  177.7 2.1 copy-start.11
  179.5 2.6 copy-start.4
  179.5 2.6 copy-start.17
  179.5 2.6 copy-start.26
  179.5 2.6 copy-start.33
where the time goes:
time: 268 us; the launch traced here: 264 us
  blocking collectives  78.6 us (29%)
  matrix products  66.9 us (25%)
  other arithmetic  53 us (20%)
  local copies, waits for them, and re-layouts  52 us (19%)
  starting transfers between devices  10.8 us (4%)
    psum x1, blocking collectives, local(): q_gain_grad, k_gain_grad = lax.psum((q_part, k_part), ('seq', 'head'))  78.6 us
    dot_general x2, matrix products, attend(): jnp.einsum('hgqk,khd->qhgd', weights, vb, preferred_element_type=jnp.floa...  17.4 us
    dot_general x2, matrix products, propagate(): jnp.einsum('qhgd,khd->hgqk', gb, vb, preferred_element_type=jnp.float32)  14 us
    mul x4, other arithmetic, norm_back(): dy = g * cosv[:, None, :] + rotate_back(g * sinv[:, None, :])  12.2 us
    ppermute x4, starting transfers between devices, shifted(): return lax.ppermute(block, axis, route)  10.8 us
    dot_general x2, matrix products, propagate(): jnp.einsum('hgqk,qhgd->khd', weights, gb, preferred_element_type=jnp.floa...  9.81 us
    dot_general x2, matrix products, propagate(): jnp.einsum('hgqk,khd->qhgd', dscore, kb, preferred_element_type=jnp.float32)  9.8 us
    unnamed x64, local copies, waits for them, and re-layouts  9.73 us
  transfers between devices with their start and end apart: 4, of which 0 were waited for; matrix products, arithmetic and copies ran while one was open for 25% of the time, Pallas kernels for 0%

commit v1 on v0

v1 whole, which is shorter than its diff:
```python
import functools

import jax
import jax.numpy as jnp
import numpy as np
from jax import lax
from jax.experimental import pallas as pl
from jax.experimental.pallas import tpu as pltpu
from jax.sharding import PartitionSpec as P

WINDOW = 1024
BLOCK = 256
SCALE = 168.0 ** (-0.5)
EPS = 1e-06
BASE = 10000.0
LOG2E = 1.4426950408889634
LN2 = 0.6931471805599453
NEG = -1e30
APART = -32768.0
NO_DOC = 64
F32 = jnp.float32
BF16 = jnp.bfloat16
NT = (((1,), (1,)), ((), ()))
NN = (((1,), (0,)), ((), ()))
TN = (((0,), (0,)), ((), ()))


def shifted(block, axis, distance):
    devices = range(lax.axis_size(axis))
    route = [(i - distance, i) for i in devices if i - distance in devices]
    return lax.ppermute(block, axis, route)


def tables(tok, devices, dim):
    half = dim // 2
    freq = BASE ** (-np.arange(half, dtype=np.float64) * 2.0 / dim)
    freq = np.concatenate([freq, freq])
    sign = np.concatenate([-np.ones(half), np.ones(half)])
    inner = np.arange(tok, dtype=np.float64)[:, None] * freq
    rows = -(-(devices + 1) // 8) * 8
    outer = (np.arange(rows, dtype=np.float64)[:, None] - 1.0) * tok * freq
    return tuple(
        np.asarray(a, np.float32)
        for a in (np.cos(inner), np.sin(inner) * sign, np.cos(outer), np.sin(outer) * sign)
    )


def dot(a, b, dims):
    return lax.dot_general(a, b, dims, preferred_element_type=F32)


def turn(cos_ref, sin_ref, cdev_ref, sdev_ref, row):
    cl, sl = cos_ref[...], sin_ref[...]
    cd, sd = cdev_ref[pl.ds(row, 1), :], sdev_ref[pl.ds(row, 1), :]
    return cl * cd - sl * sd, sl * cd + cl * sd


def swap(y):
    return pltpu.roll(y, y.shape[-1] // 2, 1)


def inverse_rms(x):
    return lax.rsqrt(jnp.mean(x * x, axis=-1, keepdims=True) + EPS)


def normed(raw, gain, cosv, sinv):
    x = raw.astype(F32)
    y = x * inverse_rms(x) * gain
    return (y * cosv + swap(y) * sinv).astype(BF16)


def unturn(g, cosv, sinv):
    return g * cosv - swap(g) * sinv


def doc_rows(seg):
    row = jnp.concatenate([seg[i : i + 1, :] for i in range(seg.shape[0])], axis=1)
    ids = lax.broadcasted_iota(jnp.int32, (128, row.shape[1]), 0)
    return jnp.where(ids == row, 1.0, 0.0).T


def query_side(onehot):
    return ((1.0 - onehot) * APART).astype(BF16)


def corner(strict):
    k = lax.broadcasted_iota(jnp.int32, (BLOCK, BLOCK), 0)
    q = lax.broadcasted_iota(jnp.int32, (BLOCK, BLOCK), 1)
    return k > q if strict else k <= q


def masked_tail(score, inside):
    edge = score.shape[0] - BLOCK
    if edge == 0:
        return jnp.where(inside, score, NEG)
    return jnp.concatenate([score[:edge], jnp.where(inside, score[edge:], NEG)], axis=0)


def masked_head(score, inside):
    if score.shape[0] == BLOCK:
        return jnp.where(inside, score, NEG)
    return jnp.concatenate([jnp.where(inside, score[:BLOCK], NEG), score[BLOCK:]], axis=0)


def stats_kernel(
    q_ref, k_ref, v_ref, g_ref, seg_ref, qgain_ref, kgain_ref, cos_ref, sin_ref, cdev_ref, sdev_ref,
    qh_ref, kh_ref, stat_ref,
):
    tok, dim = k_ref.shape
    group = q_ref.shape[1] // dim
    s = lax.axis_index("seq")
    cosv, sinv = turn(cos_ref, sin_ref, cdev_ref, sdev_ref, s + 1)
    onehot = doc_rows(seg_ref[pl.ds(s, 1)][0])
    kh = normed(k_ref[...], kgain_ref[...], cosv, sinv)
    kh_ref[...] = kh
    kside = jnp.concatenate([kh, onehot.astype(BF16)], axis=1)
    qdoc = query_side(onehot)
    inside = corner(False)
    for g in range(group):
        cols = slice(g * dim, (g + 1) * dim)
        qh = normed(q_ref[:, cols], qgain_ref[...] * (SCALE * LOG2E), cosv, sinv)
        qh_ref[:, cols] = qh
        qside = jnp.concatenate([qh, qdoc], axis=1)
        for i in range(tok // BLOCK):
            rows = slice(i * BLOCK, (i + 1) * BLOCK)
            top = (i + 1) * BLOCK
            score = dot(kside[:top], qside[rows], NT)
            score = masked_tail(score, inside)
            dprob = dot(v_ref[:top, :], g_ref[rows, cols], NT)
            m = jnp.max(score, axis=0, keepdims=True)
            e = jnp.exp2(score - m)
            stat_ref[0, g : g + 1, rows] = m
            stat_ref[0, group + g : group + g + 1, rows] = jnp.sum(e, axis=0, keepdims=True)
            stat_ref[0, 2 * group + g : 2 * group + g + 1, rows] = jnp.sum(e * dprob, axis=0, keepdims=True)


def halo_kernel(
    qh_ref, k_ref, v_ref, g_ref, seg_ref, kgain_ref, cos_ref, sin_ref, cdev_ref, sdev_ref, stat_ref,
    dq_ref, dk_ref, dv_ref, fin_ref, part_ref, ds_ref, pb_ref,
):
    tok, dim = k_ref.shape
    group = qh_ref.shape[1] // dim
    s = lax.axis_index("seq")
    cosv, sinv = turn(cos_ref, sin_ref, cdev_ref, sdev_ref, s)
    qdoc = query_side(doc_rows(seg_ref[pl.ds(s, 1)][0]))
    before = seg_ref[pl.ds(jnp.maximum(s - 1, 0), 1)][0]
    kdoc = doc_rows(jnp.where(s == 0, NO_DOC, before)).astype(BF16)
    kh = normed(k_ref[...], kgain_ref[...], cosv, sinv)
    kside = jnp.concatenate([kh, kdoc], axis=1)
    inside = corner(True)
    for g in range(group):
        cols = slice(g * dim, (g + 1) * dim)
        qside = jnp.concatenate([qh_ref[:, cols], qdoc], axis=1)
        for i in range(tok // BLOCK):
            rows = slice(i * BLOCK, (i + 1) * BLOCK)
            low = i * BLOCK
            score = dot(kside[low:], qside[rows], NT)
            score = masked_head(score, inside)
            dprob = dot(v_ref[low:, :], g_ref[rows, cols], NT)
            m_own = stat_ref[0, g : g + 1, rows]
            m = jnp.maximum(m_own, jnp.max(score, axis=0, keepdims=True))
            e = jnp.exp2(score - m)
            keep = jnp.exp2(m_own - m)
            total = stat_ref[0, group + g : group + g + 1, rows] * keep + jnp.sum(e, axis=0, keepdims=True)
            moment = stat_ref[0, 2 * group + g : 2 * group + g + 1, rows] * keep + jnp.sum(
                e * dprob, axis=0, keepdims=True
            )
            inv = 1.0 / total
            delta = moment * inv
            fin_ref[0, g : g + 1, rows] = m + jnp.log2(total)
            fin_ref[0, group + g : group + g + 1, rows] = delta
            p = e * inv
            ds = (p * (dprob - delta)).astype(BF16)
            spot = slice(g * tok + i * BLOCK, g * tok + (i + 1) * BLOCK)
            pb_ref[low:, spot] = p.astype(BF16)
            ds_ref[low:, spot] = ds
            dq_ref[rows, cols] = dot(ds, kh[low:], TN)
    part = jnp.zeros((8, dim), F32)
    for j in range(tok // BLOCK):
        rows = slice(j * BLOCK, (j + 1) * BLOCK)
        high = (j + 1) * BLOCK
        dk, dv = 0.0, 0.0
        for g in range(group):
            spot = slice(g * tok, g * tok + high)
            cols = slice(g * dim, (g + 1) * dim)
            dk = dk + dot(ds_ref[rows, spot], qh_ref[:high, cols], NN)
            dv = dv + dot(pb_ref[rows, spot], g_ref[:high, cols], NN)
        dy = unturn(dk * LN2, cosv[rows], sinv[rows])
        x = k_ref[rows, :].astype(F32)
        part = part + jnp.sum((dy * x * inverse_rms(x)).reshape(BLOCK // 8, 8, dim), axis=0)
        dk_ref[rows, :] = dy.astype(BF16)
        dv_ref[rows, :] = dv.astype(BF16)
    part_ref[0] = part


def own_kernel(
    qh_ref, kh_ref, v_ref, g_ref, q_ref, k_ref, seg_ref, qgain_ref, cos_ref, sin_ref, cdev_ref, sdev_ref,
    fin_ref, dqp_ref, qg_ref, dy_ref, dv_ref, part_ref, ds_ref, pb_ref,
):
    tok, dim = kh_ref.shape
    group = qh_ref.shape[1] // dim
    s = lax.axis_index("seq")
    cosv, sinv = turn(cos_ref, sin_ref, cdev_ref, sdev_ref, s + 1)
    onehot = doc_rows(seg_ref[pl.ds(s, 1)][0])
    kh = kh_ref[...]
    kside = jnp.concatenate([kh, onehot.astype(BF16)], axis=1)
    qdoc = query_side(onehot)
    inside = corner(False)
    gain = qgain_ref[...]
    qpart = jnp.zeros((8, dim), F32)
    for g in range(group):
        cols = slice(g * dim, (g + 1) * dim)
        qside = jnp.concatenate([qh_ref[:, cols], qdoc], axis=1)
        for i in range(tok // BLOCK):
            rows = slice(i * BLOCK, (i + 1) * BLOCK)
            top = (i + 1) * BLOCK
            score = dot(kside[:top], qside[rows], NT)
            score = masked_tail(score, inside)
            dprob = dot(v_ref[:top, :], g_ref[rows, cols], NT)
            p = jnp.exp2(score - fin_ref[0, g : g + 1, rows])
            ds = (p * (dprob - fin_ref[0, group + g : group + g + 1, rows])).astype(BF16)
            spot = slice(g * tok + i * BLOCK, g * tok + (i + 1) * BLOCK)
            pb_ref[:top, spot] = p.astype(BF16)
            ds_ref[:top, spot] = ds
            dq = dqp_ref[rows, cols] + dot(ds, kh[:top], TN)
            dy = unturn(dq * SCALE, cosv[rows], sinv[rows])
            x = q_ref[rows, cols].astype(F32)
            rstd = inverse_rms(x)
            qpart = qpart + jnp.sum((dy * x * rstd).reshape(BLOCK // 8, 8, dim), axis=0)
            gy = dy * gain
            mean = jnp.mean(gy * x, axis=-1, keepdims=True)
            qg_ref[rows, cols] = (rstd * gy - x * (rstd * rstd * rstd * mean)).astype(BF16)
    kpart = jnp.zeros((8, dim), F32)
    for j in range(tok // BLOCK):
        rows = slice(j * BLOCK, (j + 1) * BLOCK)
        low = j * BLOCK
        dk, dv = 0.0, 0.0
        for g in range(group):
            spot = slice(g * tok + low, (g + 1) * tok)
            cols = slice(g * dim, (g + 1) * dim)
            dk = dk + dot(ds_ref[rows, spot], qh_ref[low:, cols], NN)
            dv = dv + dot(pb_ref[rows, spot], g_ref[low:, cols], NN)
        dy = unturn(dk * LN2, cosv[rows], sinv[rows])
        x = k_ref[rows, :].astype(F32)
        kpart = kpart + jnp.sum((dy * x * inverse_rms(x)).reshape(BLOCK // 8, 8, dim), axis=0)
        dy_ref[rows, :] = dy
        dv_ref[rows, :] = dv
    part_ref[0, 0:8, :] = qpart
    part_ref[0, 8:16, :] = kpart


def finish_kernel(k_ref, dy_ref, dv_ref, dyb_ref, dvb_ref, kgain_ref, kg_ref, vg_ref):
    x = k_ref[...].astype(F32)
    rstd = inverse_rms(x)
    gy = (dy_ref[...] + dyb_ref[...].astype(F32)) * kgain_ref[...]
    mean = jnp.mean(gy * x, axis=-1, keepdims=True)
    kg_ref[...] = (rstd * gy - x * (rstd * rstd * rstd * mean)).astype(BF16)
    vg_ref[...] = (dv_ref[...] + dvb_ref[...].astype(F32)).astype(BF16)


def sum_all(x, work):
    done = None
    for axis in ("seq", "head"):
        size, step = lax.axis_size(axis), 1
        while step < size:
            x = x + lax.ppermute(x, axis, [(i, i ^ step) for i in range(size)])
            if axis == "seq" and step == 2:
                done = work()
                x, done = lax.optimization_barrier((x, done))
            step *= 2
    return x, done


def local(q_raw, k_raw, values, grad_out, segment_ids, q_gain, k_gain):
    tok = q_raw.shape[0]
    dim = q_gain.shape[0]
    q_local = q_raw.shape[1] // dim
    kv_local = k_raw.shape[1] // dim
    group = q_local // kv_local
    devices = lax.axis_size("seq")
    cos, sin, cdev, sdev = tables(tok, devices, dim)
    seg = segment_ids.reshape(devices, tok // 128, 128)
    qgain, kgain = q_gain.reshape(1, dim), k_gain.reshape(1, dim)

    k_prev = shifted(k_raw, "seq", 1)
    v_prev = shifted(values, "seq", 1)

    def whole(a):
        return pl.BlockSpec(a.shape, lambda h: (0,) * a.ndim)

    qspec = pl.BlockSpec((tok, group * dim), lambda h: (0, h))
    kspec = pl.BlockSpec((tok, dim), lambda h: (0, h))
    stat_spec = pl.BlockSpec((1, 8, tok), lambda h: (h, 0, 0))
    stat_shape = jax.ShapeDtypeStruct((kv_local, 8, tok), F32)
    turns = (cos, sin, cdev, sdev)
    turn_specs = [whole(a) for a in turns]
    params = pltpu.CompilerParams(vmem_limit_bytes=60 * 1024 * 1024)
    scratch = [pltpu.VMEM((tok, group * tok), BF16)] * 2

    def cost(products):
        pairs = q_local * tok * tok * 5 // 8
        return pl.CostEstimate(
            flops=2 * products * pairs * dim * 2, bytes_accessed=4 << 20, transcendentals=pairs
        )

    qh, kh, stat = pl.pallas_call(
        stats_kernel,
        grid=(kv_local,),
        in_specs=[qspec, kspec, kspec, qspec, whole(seg), whole(qgain), whole(kgain)] + turn_specs,
        out_specs=[qspec, kspec, stat_spec],
        out_shape=[
            jax.ShapeDtypeStruct(q_raw.shape, BF16),
            jax.ShapeDtypeStruct(k_raw.shape, BF16),
            stat_shape,
        ],
        compiler_params=params,
        cost_estimate=cost(2),
        name="own_statistics",
    )(q_raw, k_raw, values, grad_out, seg, qgain, kgain, *turns)

    dq_prev, dk_prev, dv_prev, fin, kpart_prev = pl.pallas_call(
        halo_kernel,
        grid=(kv_local,),
        in_specs=[qspec, kspec, kspec, qspec, whole(seg), whole(kgain)] + turn_specs + [stat_spec],
        out_specs=[qspec, kspec, kspec, stat_spec, pl.BlockSpec((1, 8, dim), lambda h: (h, 0, 0))],
        out_shape=[
            jax.ShapeDtypeStruct(q_raw.shape, F32),
            jax.ShapeDtypeStruct(k_raw.shape, BF16),
            jax.ShapeDtypeStruct(k_raw.shape, BF16),
            stat_shape,
            jax.ShapeDtypeStruct((kv_local, 8, dim), F32),
        ],
        scratch_shapes=scratch,
        compiler_params=params,
        cost_estimate=cost(5),
        name="previous_keys",
    )(qh, k_prev, v_prev, grad_out, seg, kgain, *turns, stat)

    dy_back = shifted(dk_prev, "seq", -1)
    dv_back = shifted(dv_prev, "seq", -1)

    q_grad, dy_own, dv_own, parts = pl.pallas_call(
        own_kernel,
        grid=(kv_local,),
        in_specs=[qspec, kspec, kspec, qspec, qspec, kspec, whole(seg), whole(qgain)]
        + turn_specs
        + [stat_spec, qspec],
        out_specs=[qspec, kspec, kspec, pl.BlockSpec((1, 16, dim), lambda h: (h, 0, 0))],
        out_shape=[
            jax.ShapeDtypeStruct(q_raw.shape, BF16),
            jax.ShapeDtypeStruct(k_raw.shape, F32),
            jax.ShapeDtypeStruct(k_raw.shape, F32),
            jax.ShapeDtypeStruct((kv_local, 16, dim), F32),
        ],
        scratch_shapes=scratch,
        compiler_params=params,
        cost_estimate=cost(5),
        name="own_keys",
    )(qh, kh, values, grad_out, q_raw, k_raw, seg, qgain, *turns, fin, dq_prev)

    sums = jnp.stack(
        [jnp.sum(parts[:, :8], axis=(0, 1)), jnp.sum(parts[:, 8:], axis=(0, 1)) + jnp.sum(kpart_prev, axis=(0, 1))]
    )
    sums, dy_back, dv_back = lax.optimization_barrier((sums, dy_back, dv_back))

    finish = pl.pallas_call(
        finish_kernel,
        grid=(kv_local,),
        in_specs=[kspec] * 5 + [whole(kgain)],
        out_specs=[kspec, kspec],
        out_shape=[jax.ShapeDtypeStruct(k_raw.shape, BF16)] * 2,
        compiler_params=params,
        cost_estimate=pl.CostEstimate(flops=1 << 20, bytes_accessed=5 << 20, transcendentals=0),
        name="add_returned",
    )
    sums, (k_grad, v_grad) = sum_all(
        sums, lambda: finish(k_raw, dy_own, dv_own, dy_back, dv_back, kgain)
    )
    return (q_grad, k_grad, v_grad, sums[0], sums[1])


def solution(mesh):
    in_specs = (
        P("seq", "head"),
        P("seq", "head"),
        P("seq", "head"),
        P("seq", "head"),
        P(),
        P(),
        P(),
    )
    out_specs = (P("seq", "head"), P("seq", "head"), P("seq", "head"), P(), P())
    return jax.shard_map(local, mesh=mesh, in_specs=in_specs, out_specs=out_specs, check_vma=False)
```

time: 268 us -> 96.5 us (0.36); the launches traced: 264 us -> 96.2 us
  blocking collectives: 78.6 us -> 0 us
  matrix products: 66.9 us -> 0 us
  other arithmetic: 53 us -> 0.79 us
  local copies, waits for them, and re-layouts: 52 us -> 1.47 us
  Pallas kernels: 0 us -> 48.4 us
  starting transfers between devices: 10.8 us -> 29.1 us
  waiting for transfers between devices: 0.01 us -> 15.7 us
    psum x1 -> x0, blocking collectives: 78.6 us -> none  [local(): q_gain_grad, k_gain_grad = lax.psum((q_part, k_part), ('seq', 'head'))]
    dot_general x12 -> x0, matrix products: 66.9 us -> none  [the longest x2 17.4 us: attend(): jnp.einsum('hgqk,khd->qhgd', weights, vb, preferred_element_type=jnp.floa...]
    pallas_call x0 -> x4, Pallas kernels: none -> 48.4 us  [the longest x1 19 us: local(): pl.pallas_call(halo_kernel, grid=(kv_local,), in_specs=[qspec, kspec, ksp...]
    ppermute x0 -> x8, starting transfers between devices: none -> 18.9 us  [sum_all(): x = x + lax.ppermute(x, axis, [(i, i ^ step) for i in range(size)])]
    ppermute x0 -> x8, waiting for transfers between devices: none -> 15.7 us  [sum_all(): x = x + lax.ppermute(x, axis, [(i, i ^ step) for i in range(size)])]
    mul x8 -> x0, other arithmetic: 13.2 us -> none  [the longest x4 12.2 us: norm_back(): dy = g * cosv[:, None, :] + rotate_back(g * sinv[:, None, :])]
    convert_element_type x7 -> x0, other arithmetic: 12.2 us -> none  [the longest x2 7.18 us: normed(): return (out.astype(jnp.bfloat16), rstd)]
    dynamic_slice x17 -> x0, local copies, waits for them, and re-layouts: 9.28 us -> none  [the longest x4 7.51 us: step(): gb = lax.dynamic_slice_in_dim(grads, first, BLOCK)]
  transfers between devices with their start and end apart: 4 -> 12, of which waited for: 0 -> 8; matrix products, arithmetic and copies ran while one was open for 25% -> 1% of each run, Pallas kernels for 0% -> 31%
where the time goes in v1:
time: 96.5 us; the launch traced here: 96.2 us
  Pallas kernels  48.4 us (50%)
  starting transfers between devices  29.1 us (30%)
  waiting for transfers between devices  15.7 us (16%)
  local copies, waits for them, and re-layouts  1.47 us (2%)
    pallas_call x1, Pallas kernels, local(): pl.pallas_call(halo_kernel, grid=(kv_local,), in_specs=[qspec, kspec, ksp...  19 us
    ppermute x8, starting transfers between devices, sum_all(): x = x + lax.ppermute(x, axis, [(i, i ^ step) for i in range(size)])  18.9 us
    ppermute x8, waiting for transfers between devices, sum_all(): x = x + lax.ppermute(x, axis, [(i, i ^ step) for i in range(size)])  15.7 us
    pallas_call x1, Pallas kernels, local(): pl.pallas_call(own_kernel, grid=(kv_local,), in_specs=[qspec, kspec, kspe...  14.6 us
    pallas_call x1, Pallas kernels, local(): pl.pallas_call(stats_kernel, grid=(kv_local,), in_specs=[qspec, kspec, ks...  11.7 us
    ppermute x4, starting transfers between devices, shifted(): return lax.ppermute(block, axis, route)  10.1 us
    pallas_call x1, Pallas kernels, local(): finish(k_raw, dy_own, dv_own, dy_back, dv_back, kgain)  3.16 us
  transfers between devices with their start and end apart: 12, of which 8 were waited for; matrix products, arithmetic and copies ran while one was open for 1% of the time, Pallas kernels for 31%

profile of v1, /device:TPU:14, one launch (start us, length us, event | category | flops | bytes accessed | tf_op | source)
XLA Modules:
  0.0 96.2 jit_solution(10186009524602972912)
XLA Ops:
  0.6 1.9 %collective-permute-start.1 = (bf16[1024,256]{1,0:T(8,128)(2,1)}, bf16[1024,256]{1,0:T(8,128)(2,1)S(1)}, u32[]{:S(2)}, u32[]{:S(2)}) collective-permute-start(bf16[1024,256]{1,0:T(8,128)(2,1)} %v_ref.3), channel_id=1, source_target_pairs={{0,8},{8,16},{16,24},{24,32},{32,40},{40,48},{48,56},{56,64},{64,7... | collective-permute-start | bytes 1572872 | tf_op jit(solution)/shard_map/ppermute | solution.py:31
  2.6 4.2 %collective-permute-start = (bf16[1024,256]{1,0:T(8,128)(2,1)}, bf16[1024,256]{1,0:T(8,128)(2,1)S(1)}, u32[]{:S(2)}, u32[]{:S(2)}) collective-permute-start(bf16[1024,256]{1,0:T(8,128)(2,1)} %k_ref.5), channel_id=1, source_target_pairs={{0,8},{8,16},{16,24},{24,32},{32,40},{40,48},{48,56},{56,64},{64,7... | collective-permute-start | bytes 1572872 | tf_op jit(solution)/shard_map/ppermute | solution.py:31
  6.8 11.7 %own_statistics.1 = (bf16[1024,512]{1,0:T(8,128)(2,1)}, bf16[1024,256]{1,0:T(8,128)(2,1)}, f32[2,8,1024]{2,1,0:T(8,128)}) custom-call(bf16[1024,512]{1,0:T(8,128)(2,1)} %q_ref.3, bf16[1024,256]{1,0:T(8,128)(2,1)} %k_ref.5, bf16[1024,256]{1,0:T(8,128)(2,1)} %v_ref.3, bf16[1024,512]{1,0:T(8,128)(2,1)} %g_ref.5, s32[32,8,128]{2,1,0:T(8,128)} %bitcast.14, ...), custom_call_target="tpu_custom_call" | custom-call | flops 2684354560 | bytes 4194304 | tf_op jit(solution)/shard_map/own_statistics/pallas_call | solution.py:306
  18.5 0.0 collective-permute-done.1.v_ref
  18.5 0.0 copy-start.3
  18.5 0.0 collective-permute-done.k_ref
  18.5 0.0 copy-start.4
  18.5 0.8 copy-done.3
  19.3 0.2 copy-done.4
  19.4 19.0 %previous_keys.1 = (f32[1024,512]{1,0:T(8,128)}, bf16[1024,256]{1,0:T(8,128)(2,1)}, bf16[1024,256]{1,0:T(8,128)(2,1)}, f32[2,8,1024]{2,1,0:T(8,128)}, f32[2,8,128]{2,1,0:T(8,128)}) custom-call(bf16[1024,512]{1,0:T(8,128)(2,1)} %get-tuple-element.25.qh_ref, bf16[1024,256]{1,0:T(8,128)(2,1)} %copy-done.4, bf16[1024,256]{1,0:T(8,128)(2,1)} %copy-done.3, ...), custom_call_target="tpu_custom_call" | custom-call | flops 6710886400 | bytes 4194304 | tf_op jit(solution)/shard_map/previous_keys/pallas_call | solution.py:321
  38.4 1.9 %collective-permute-start.2 = (bf16[1024,256]{1,0:T(8,128)(2,1)}, bf16[1024,256]{1,0:T(8,128)(2,1)S(1)}, u32[]{:S(2)}, u32[]{:S(2)}) collective-permute-start(bf16[1024,256]{1,0:T(8,128)(2,1)} %get-tuple-element.33), channel_id=1, source_target_pairs={{8,0},{16,8},{24,16},{32,24},{40,32},{48,40},{56,48},{64,56},{72,6... | collective-permute-start | bytes 1572872 | tf_op jit(solution)/shard_map/ppermute | solution.py:31
  40.3 2.1 %collective-permute-start.3 = (bf16[1024,256]{1,0:T(8,128)(2,1)}, bf16[1024,256]{1,0:T(8,128)(2,1)S(1)}, u32[]{:S(2)}, u32[]{:S(2)}) collective-permute-start(bf16[1024,256]{1,0:T(8,128)(2,1)} %get-tuple-element.34), channel_id=1, source_target_pairs={{8,0},{16,8},{24,16},{32,24},{40,32},{48,40},{56,48},{64,56},{72,6... | collective-permute-start | bytes 1572872 | tf_op jit(solution)/shard_map/ppermute | solution.py:31
  42.4 0.0 copy-start.2
  42.5 14.6 %own_keys.1 = (bf16[1024,512]{1,0:T(8,128)(2,1)}, f32[1024,256]{1,0:T(8,128)}, f32[1024,256]{1,0:T(8,128)}, f32[2,16,128]{2,1,0:T(8,128)}) custom-call(bf16[1024,512]{1,0:T(8,128)(2,1)} %get-tuple-element.25.qh_ref, bf16[1024,256]{1,0:T(8,128)(2,1)} %get-tuple-element.26.kh_ref, bf16[1024,256]{1,0:T(8,128)(2,1)} %v_ref.3, bf16[1024,512]{1,0:T(8,128)(2,1)} %g_ref.5, ...), custom_call_target="tpu_custom_call" | custom-call | flops 6710886400 | bytes 4194304 | tf_op jit(solution)/shard_map/own_keys/pallas_call | solution.py:342
  57.0 0.0 copy-done.2
  57.0 0.7 slice_reduce_fusion.1
  57.8 0.0 collective-permute-done.2.dyb_ref
  57.8 0.0 copy-start
  57.8 0.0 collective-permute-done.3.dvb_ref
  57.8 0.0 copy-start.1
  57.8 0.6 collective-permute-start.4
  58.4 0.8 collective-permute-done.4
  59.2 0.0 collective-permute-start.5
  59.2 0.0 copy-done
  59.2 0.0 copy-done.1
  59.3 3.2 %add_returned.1 = (bf16[1024,256]{1,0:T(8,128)(2,1)}, bf16[1024,256]{1,0:T(8,128)(2,1)}) custom-call(bf16[1024,256]{1,0:T(8,128)(2,1)} %k_ref.5, f32[1024,256]{1,0:T(8,128)} %get-tuple-element.36.dy_ref, f32[1024,256]{1,0:T(8,128)} %get-tuple-element.37.dv_ref, bf16[1024,256]{1,0:T(8,128)(2,1)} %copy-done, bf16[1024,256]{1,0:T(8,128)(2,1)} %copy-done.1, ...), custom_call_target="tpu_custom_call" | custom-call | flops 1048576 | bytes 5242880 | tf_op jit(solution)/shard_map/add_returned/pallas_call | solution.py:377
  62.4 0.4 collective-permute-done.5
  62.8 3.1 %collective-permute-start.6 = (f32[2,128]{1,0:T(2,128)S(1)}, f32[2,128]{1,0:T(2,128)S(1)}, u32[]{:S(2)}, u32[]{:S(2)}) collective-permute-start(f32[2,128]{1,0:T(2,128)S(1)} %add.40), channel_id=1, source_target_pairs={{0,32},{8,40},{16,48},{24,56},{32,0},{40,8},{48,16},{56,24},{64,96... | collective-permute-start | bytes 3080 | tf_op jit(solution)/shard_map/ppermute | solution.py:266
  65.9 1.5 %collective-permute-done.6 = f32[2,128]{1,0:T(2,128)S(1)} collective-permute-done((f32[2,128]{1,0:T(2,128)S(1)}, f32[2,128]{1,0:T(2,128)S(1)}, u32[]{:S(2)}, u32[]{:S(2)}) %collective-permute-start.6) | collective-permute-done | bytes 1056 | tf_op jit(solution)/shard_map/ppermute | solution.py:266
  67.4 3.4 %collective-permute-start.7 = (f32[2,128]{1,0:T(2,128)S(1)}, f32[2,128]{1,0:T(2,128)S(1)}, u32[]{:S(2)}, u32[]{:S(2)}) collective-permute-start(f32[2,128]{1,0:T(2,128)S(1)} %add.41), channel_id=1, source_target_pairs={{0,64},{8,72},{16,80},{24,88},{32,96},{40,104},{48,112},{56,120},{... | collective-permute-start | bytes 3080 | tf_op jit(solution)/shard_map/ppermute | solution.py:266
  70.8 1.5 %collective-permute-done.7 = f32[2,128]{1,0:T(2,128)S(1)} collective-permute-done((f32[2,128]{1,0:T(2,128)S(1)}, f32[2,128]{1,0:T(2,128)S(1)}, u32[]{:S(2)}, u32[]{:S(2)}) %collective-permute-start.7) | collective-permute-done | bytes 1056 | tf_op jit(solution)/shard_map/ppermute | solution.py:266
  72.4 8.1 %collective-permute-start.8 = (f32[2,128]{1,0:T(2,128)S(1)}, f32[2,128]{1,0:T(2,128)S(1)}, u32[]{:S(2)}, u32[]{:S(2)}) collective-permute-start(f32[2,128]{1,0:T(2,128)S(1)} %add.42), channel_id=1, source_target_pairs={{0,128},{8,136},{16,144},{24,152},{32,160},{40,168},{48,176},{56,1... | collective-permute-start | bytes 3080 | tf_op jit(solution)/shard_map/ppermute | solution.py:266
  80.4 1.5 %collective-permute-done.8 = f32[2,128]{1,0:T(2,128)S(1)} collective-permute-done((f32[2,128]{1,0:T(2,128)S(1)}, f32[2,128]{1,0:T(2,128)S(1)}, u32[]{:S(2)}, u32[]{:S(2)}) %collective-permute-start.8) | collective-permute-done | bytes 1056 | tf_op jit(solution)/shard_map/ppermute | solution.py:266
  82.0 0.4 collective-permute-start.9
  82.4 3.1 %collective-permute-done.9 = f32[2,128]{1,0:T(2,128)S(1)} collective-permute-done((f32[2,128]{1,0:T(2,128)S(1)}, f32[2,128]{1,0:T(2,128)S(1)}, u32[]{:S(2)}, u32[]{:S(2)}) %collective-permute-start.9) | collective-permute-done | bytes 1056 | tf_op jit(solution)/shard_map/ppermute | solution.py:266
  85.5 2.3 %collective-permute-start.10 = (f32[2,128]{1,0:T(2,128)S(1)}, f32[2,128]{1,0:T(2,128)S(1)}, u32[]{:S(2)}, u32[]{:S(2)}) collective-permute-start(f32[2,128]{1,0:T(2,128)S(1)} %add.44), channel_id=1, source_target_pairs={{0,2},{1,3},{2,0},{3,1},{4,6},{5,7},{6,4},{7,5},{8,10},{9,11},{10,... | collective-permute-start | bytes 3080 | tf_op jit(solution)/shard_map/ppermute | solution.py:266
  87.8 2.8 %collective-permute-done.10 = f32[2,128]{1,0:T(2,128)S(1)} collective-permute-done((f32[2,128]{1,0:T(2,128)S(1)}, f32[2,128]{1,0:T(2,128)S(1)}, u32[]{:S(2)}, u32[]{:S(2)}) %collective-permute-start.10) | collective-permute-done | bytes 1056 | tf_op jit(solution)/shard_map/ppermute | solution.py:266
  90.6 1.1 %collective-permute-start.11 = (f32[2,128]{1,0:T(2,128)S(1)}, f32[2,128]{1,0:T(2,128)S(1)}, u32[]{:S(2)}, u32[]{:S(2)}) collective-permute-start(f32[2,128]{1,0:T(2,128)S(1)} %add.45), channel_id=1, source_target_pairs={{0,4},{1,5},{2,6},{3,7},{4,0},{5,1},{6,2},{7,3},{8,12},{9,13},{10,... | collective-permute-start | bytes 3080 | tf_op jit(solution)/shard_map/ppermute | solution.py:266
  91.7 4.0 %collective-permute-done.11 = f32[2,128]{1,0:T(2,128)S(1)} collective-permute-done((f32[2,128]{1,0:T(2,128)S(1)}, f32[2,128]{1,0:T(2,128)S(1)}, u32[]{:S(2)}, u32[]{:S(2)}) %collective-permute-start.11) | collective-permute-done | bytes 1056 | tf_op jit(solution)/shard_map/ppermute | solution.py:266
  95.7 0.5 slice_bitcast_fusion
  (11 shorter events, 0.1 us)
Async XLA Ops:
  0.6 17.8 %collective-permute-start.1 = (bf16[1024,256]{1,0:T(8,128)(2,1)}, bf16[1024,256]{1,0:T(8,128)(2,1)S(1)}, u32[]{:S(2)}, u32[]{:S(2)}) collective-permute-start(bf16[1024,256]{1,0:T(8,128)(2,1)} %v_ref.3), channel_id=1, source_target_pairs={{0,8},{8,16},{16,24},{24,32},{32,40},{40,48},{48,56},{56,64},{64,7... | collective-permute-start | bytes 1572872 | tf_op jit(solution)/shard_map/ppermute | solution.py:31
  2.6 15.9 %collective-permute-start = (bf16[1024,256]{1,0:T(8,128)(2,1)}, bf16[1024,256]{1,0:T(8,128)(2,1)S(1)}, u32[]{:S(2)}, u32[]{:S(2)}) collective-permute-start(bf16[1024,256]{1,0:T(8,128)(2,1)} %k_ref.5), channel_id=1, source_target_pairs={{0,8},{8,16},{16,24},{24,32},{32,40},{40,48},{48,56},{56,64},{64,7... | collective-permute-start | bytes 1572872 | tf_op jit(solution)/shard_map/ppermute | solution.py:31
  18.5 0.8 copy-start.3
  18.5 0.9 copy-start.4
  38.4 19.4 %collective-permute-start.2 = (bf16[1024,256]{1,0:T(8,128)(2,1)}, bf16[1024,256]{1,0:T(8,128)(2,1)S(1)}, u32[]{:S(2)}, u32[]{:S(2)}) collective-permute-start(bf16[1024,256]{1,0:T(8,128)(2,1)} %get-tuple-element.33), channel_id=1, source_target_pairs={{8,0},{16,8},{24,16},{32,24},{40,32},{48,40},{56,48},{64,56},{72,6... | collective-permute-start | bytes 1572872 | tf_op jit(solution)/shard_map/ppermute | solution.py:31
  40.3 17.5 %collective-permute-start.3 = (bf16[1024,256]{1,0:T(8,128)(2,1)}, bf16[1024,256]{1,0:T(8,128)(2,1)S(1)}, u32[]{:S(2)}, u32[]{:S(2)}) collective-permute-start(bf16[1024,256]{1,0:T(8,128)(2,1)} %get-tuple-element.34), channel_id=1, source_target_pairs={{8,0},{16,8},{24,16},{32,24},{40,32},{48,40},{56,48},{64,56},{72,6... | collective-permute-start | bytes 1572872 | tf_op jit(solution)/shard_map/ppermute | solution.py:31
  42.4 14.6 %copy-start.2 = (f32[2,8,128]{2,1,0:T(8,128)S(1)}, f32[2,8,128]{2,1,0:T(8,128)}, u32[]{:S(2)}) copy-start(f32[2,8,128]{2,1,0:T(8,128)} %get-tuple-element.32) | copy-start | bytes 24580
  57.8 1.4 %copy-start = (bf16[1024,256]{1,0:T(8,128)(2,1)}, bf16[1024,256]{1,0:T(8,128)(2,1)S(1)}, u32[]{:S(2)}) copy-start(bf16[1024,256]{1,0:T(8,128)(2,1)S(1)} %collective-permute-done.2.dyb_ref) | copy-start | bytes 1572868
  57.8 1.4 %copy-start.1 = (bf16[1024,256]{1,0:T(8,128)(2,1)}, bf16[1024,256]{1,0:T(8,128)(2,1)S(1)}, u32[]{:S(2)}) copy-start(bf16[1024,256]{1,0:T(8,128)(2,1)S(1)} %collective-permute-done.3.dvb_ref) | copy-start | bytes 1572868
  57.8 1.4 %collective-permute-start.4 = (f32[2,128]{1,0:T(2,128)S(1)}, f32[2,128]{1,0:T(2,128)S(1)}, u32[]{:S(2)}, u32[]{:S(2)}) collective-permute-start(f32[2,128]{1,0:T(2,128)S(1)} %pad_maximum_fusion), channel_id=1, source_target_pairs={{0,8},{8,0},{16,24},{24,16},{32,40},{40,32},{48,56},{56,48},{64,72... | collective-permute-start | bytes 3080 | tf_op jit(solution)/shard_map/ppermute | solution.py:266
  59.2 3.6 %collective-permute-start.5 = (f32[2,128]{1,0:T(2,128)S(1)}, f32[2,128]{1,0:T(2,128)S(1)}, u32[]{:S(2)}, u32[]{:S(2)}) collective-permute-start(f32[2,128]{1,0:T(2,128)S(1)} %add.39), channel_id=1, source_target_pairs={{0,16},{8,24},{16,0},{24,8},{32,48},{40,56},{48,32},{56,40},{64,80... | collective-permute-start | bytes 3080 | tf_op jit(solution)/shard_map/ppermute | solution.py:266
  62.8 4.6 %collective-permute-start.6 = (f32[2,128]{1,0:T(2,128)S(1)}, f32[2,128]{1,0:T(2,128)S(1)}, u32[]{:S(2)}, u32[]{:S(2)}) collective-permute-start(f32[2,128]{1,0:T(2,128)S(1)} %add.40), channel_id=1, source_target_pairs={{0,32},{8,40},{16,48},{24,56},{32,0},{40,8},{48,16},{56,24},{64,96... | collective-permute-start | bytes 3080 | tf_op jit(solution)/shard_map/ppermute | solution.py:266
  67.4 4.9 %collective-permute-start.7 = (f32[2,128]{1,0:T(2,128)S(1)}, f32[2,128]{1,0:T(2,128)S(1)}, u32[]{:S(2)}, u32[]{:S(2)}) collective-permute-start(f32[2,128]{1,0:T(2,128)S(1)} %add.41), channel_id=1, source_target_pairs={{0,64},{8,72},{16,80},{24,88},{32,96},{40,104},{48,112},{56,120},{... | collective-permute-start | bytes 3080 | tf_op jit(solution)/shard_map/ppermute | solution.py:266
  72.4 9.6 %collective-permute-start.8 = (f32[2,128]{1,0:T(2,128)S(1)}, f32[2,128]{1,0:T(2,128)S(1)}, u32[]{:S(2)}, u32[]{:S(2)}) collective-permute-start(f32[2,128]{1,0:T(2,128)S(1)} %add.42), channel_id=1, source_target_pairs={{0,128},{8,136},{16,144},{24,152},{32,160},{40,168},{48,176},{56,1... | collective-permute-start | bytes 3080 | tf_op jit(solution)/shard_map/ppermute | solution.py:266
  82.0 3.6 %collective-permute-start.9 = (f32[2,128]{1,0:T(2,128)S(1)}, f32[2,128]{1,0:T(2,128)S(1)}, u32[]{:S(2)}, u32[]{:S(2)}) collective-permute-start(f32[2,128]{1,0:T(2,128)S(1)} %add.43), channel_id=1, source_target_pairs={{0,1},{1,0},{2,3},{3,2},{4,5},{5,4},{6,7},{7,6},{8,9},{9,8},{10,11... | collective-permute-start | bytes 3080 | tf_op jit(solution)/shard_map/ppermute | solution.py:266
  85.5 5.1 %collective-permute-start.10 = (f32[2,128]{1,0:T(2,128)S(1)}, f32[2,128]{1,0:T(2,128)S(1)}, u32[]{:S(2)}, u32[]{:S(2)}) collective-permute-start(f32[2,128]{1,0:T(2,128)S(1)} %add.44), channel_id=1, source_target_pairs={{0,2},{1,3},{2,0},{3,1},{4,6},{5,7},{6,4},{7,5},{8,10},{9,11},{10,... | collective-permute-start | bytes 3080 | tf_op jit(solution)/shard_map/ppermute | solution.py:266
  90.6 5.1 %collective-permute-start.11 = (f32[2,128]{1,0:T(2,128)S(1)}, f32[2,128]{1,0:T(2,128)S(1)}, u32[]{:S(2)}, u32[]{:S(2)}) collective-permute-start(f32[2,128]{1,0:T(2,128)S(1)} %add.45), channel_id=1, source_target_pairs={{0,4},{1,5},{2,6},{3,7},{4,0},{5,1},{6,2},{7,3},{8,12},{9,13},{10,... | collective-permute-start | bytes 3080 | tf_op jit(solution)/shard_map/ppermute | solution.py:266

commit v2 on v1

v2 whole, which is shorter than its diff:
```python
import functools

import jax
import jax.numpy as jnp
import numpy as np
from jax import lax
from jax.experimental import pallas as pl
from jax.experimental.pallas import tpu as pltpu
from jax.sharding import PartitionSpec as P

WINDOW = 1024
BLOCK = 256
SCALE = 168.0 ** (-0.5)
EPS = 1e-06
BASE = 10000.0
LOG2E = 1.4426950408889634
LN2 = 0.6931471805599453
NEG = -1e30
APART = -32768.0
DOCS = 32
F32 = jnp.float32
BF16 = jnp.bfloat16
NT = (((1,), (1,)), ((), ()))
NN = (((1,), (0,)), ((), ()))
TN = (((0,), (0,)), ((), ()))


def shifted(block, axis, distance):
    devices = range(lax.axis_size(axis))
    route = [(i - distance, i) for i in devices if i - distance in devices]
    return lax.ppermute(block, axis, route)


def tables(tok, devices, dim):
    half = dim // 2
    freq = BASE ** (-np.arange(half, dtype=np.float64) * 2.0 / dim)
    freq = np.concatenate([freq, freq])
    sign = np.concatenate([-np.ones(half), np.ones(half)])
    inner = np.arange(tok, dtype=np.float64)[:, None] * freq
    rows = -(-(devices + 1) // 8) * 8
    outer = (np.arange(rows, dtype=np.float64)[:, None] - 1.0) * tok * freq
    return tuple(
        np.asarray(a, np.float32)
        for a in (np.cos(inner), np.sin(inner) * sign, np.cos(outer), np.sin(outer) * sign)
    )


def dot(a, b, dims):
    return lax.dot_general(a, b, dims, preferred_element_type=F32)


def turn(cos_ref, sin_ref, cdev_ref, sdev_ref, row):
    cl, sl = cos_ref[...], sin_ref[...]
    cd, sd = cdev_ref[pl.ds(row, 1), :], sdev_ref[pl.ds(row, 1), :]
    return cl * cd - sl * sd, sl * cd + cl * sd


def swap(y):
    return pltpu.roll(y, y.shape[-1] // 2, 1)


def inverse_rms(x):
    return lax.rsqrt(jnp.mean(x * x, axis=-1, keepdims=True) + EPS)


def normed(raw, gain, cosv, sinv):
    x = raw.astype(F32)
    y = x * inverse_rms(x) * gain
    return (y * cosv + swap(y) * sinv).astype(BF16)


def unturn(g, cosv, sinv):
    return g * cosv - swap(g) * sinv


def doc_rows(seg):
    row = jnp.concatenate([seg[i : i + 1, :] for i in range(seg.shape[0])], axis=1)
    ids = lax.broadcasted_iota(jnp.int32, (DOCS, row.shape[1]), 0)
    return jnp.where(ids == row, 1.0, 0.0).T


def query_side(onehot):
    return ((1.0 - onehot) * APART).astype(BF16)


def corner(strict, repeat=1):
    k = lax.broadcasted_iota(jnp.int32, (BLOCK, BLOCK), 0)
    q = lax.broadcasted_iota(jnp.int32, (BLOCK, BLOCK), 1)
    inside = jnp.where(k > q if strict else k <= q, 1, 0)
    return jnp.concatenate([inside] * repeat, axis=1) > 0


def masked_tail(score, inside):
    edge = score.shape[0] - BLOCK
    if edge == 0:
        return jnp.where(inside, score, NEG)
    return jnp.concatenate([score[:edge], jnp.where(inside, score[edge:], NEG)], axis=0)


def masked_head(score, inside):
    if score.shape[0] == BLOCK:
        return jnp.where(inside, score, NEG)
    return jnp.concatenate([jnp.where(inside, score[:BLOCK], NEG), score[BLOCK:]], axis=0)


def add_up(ref, low, value, fresh):
    for j in range(value.shape[0] // BLOCK):
        rows, part = pl.ds(low + j * BLOCK, BLOCK), value[j * BLOCK : (j + 1) * BLOCK]
        ref[rows, :] = part if j == fresh else ref[rows, :] + part


def heads(ref, rows, group):
    dim = ref.shape[1] // group
    return jnp.concatenate([ref[rows, g * dim : (g + 1) * dim] for g in range(group)], axis=0)


def query_rows(ref, first, rows, group):
    return jnp.concatenate([ref[0, first + g : first + g + 1, rows] for g in range(group)], axis=1)


def stats_kernel(
    q_ref, k_ref, v_ref, g_ref, seg_ref, qgain_ref, kgain_ref, cos_ref, sin_ref, cdev_ref, sdev_ref,
    qh_ref, kh_ref, stat_ref, cosv_ref, sinv_ref, kdoc_ref, qt_ref, gt_ref,
):
    tok, dim = k_ref.shape
    group = q_ref.shape[1] // dim

    @pl.when(pl.program_id(0) == 0)
    def _():
        s = lax.axis_index("seq")
        cosv_ref[...], sinv_ref[...] = turn(cos_ref, sin_ref, cdev_ref, sdev_ref, s + 1)
        onehot = doc_rows(seg_ref[pl.ds(s, 1)][0])
        kdoc_ref[...] = onehot.astype(BF16)
        qt_ref[dim:, :] = query_side(onehot).T

    cosv, sinv = cosv_ref[...], sinv_ref[...]
    kh = normed(k_ref[...], kgain_ref[...], cosv, sinv)
    kh_ref[...] = kh
    kside = jnp.concatenate([kh, kdoc_ref[...]], axis=1)
    inside = corner(False)
    for g in range(group):
        cols = slice(g * dim, (g + 1) * dim)
        qh = normed(q_ref[:, cols], qgain_ref[...] * (SCALE * LOG2E), cosv, sinv)
        qh_ref[:, cols] = qh
        qt_ref[:dim, :] = qh.T
        gt_ref[...] = g_ref[:, cols].T
        for i in range(tok // BLOCK):
            rows = slice(i * BLOCK, (i + 1) * BLOCK)
            top = (i + 1) * BLOCK
            score = masked_tail(dot(kside[:top], qt_ref[:, rows], NN), inside)
            dprob = dot(v_ref[:top, :], gt_ref[:, rows], NN)
            m = jnp.max(score, axis=0, keepdims=True)
            e = jnp.exp2(score - m)
            stat_ref[0, g : g + 1, rows] = m
            stat_ref[0, group + g : group + g + 1, rows] = jnp.sum(e, axis=0, keepdims=True)
            stat_ref[0, 2 * group + g : 2 * group + g + 1, rows] = jnp.sum(e * dprob, axis=0, keepdims=True)


def halo_kernel(
    qh_ref, k_ref, v_ref, g_ref, seg_ref, kgain_ref, cos_ref, sin_ref, cdev_ref, sdev_ref, stat_ref,
    dq_ref, back_ref, fin_ref, part_ref, cosv_ref, sinv_ref, kdoc_ref, qdoc_ref, dka_ref, dva_ref,
):
    tok, dim = k_ref.shape
    group = qh_ref.shape[1] // dim

    @pl.when(pl.program_id(0) == 0)
    def _():
        s = lax.axis_index("seq")
        cosv_ref[...], sinv_ref[...] = turn(cos_ref, sin_ref, cdev_ref, sdev_ref, s)
        qdoc_ref[...] = query_side(doc_rows(seg_ref[pl.ds(s, 1)][0]))
        before = doc_rows(seg_ref[pl.ds(jnp.maximum(s - 1, 0), 1)][0])
        kdoc_ref[...] = jnp.where(s == 0, 1.0, before).astype(BF16)

    cosv, sinv = cosv_ref[...], sinv_ref[...]
    qdoc = qdoc_ref[...]
    kh = normed(k_ref[...], kgain_ref[...], cosv, sinv)
    kside = jnp.concatenate([kh, kdoc_ref[...]], axis=1)
    inside = corner(True, group)

    def products(i):
        rows, low = slice(i * BLOCK, (i + 1) * BLOCK), i * BLOCK
        qside = jnp.concatenate([heads(qh_ref, rows, group), jnp.concatenate([qdoc[rows]] * group, axis=0)], axis=1)
        return dot(kside[low:], qside, NT), dot(v_ref[low:, :], heads(g_ref, rows, group), NT)

    def soft(i, score, dprob):
        rows = slice(i * BLOCK, (i + 1) * BLOCK)
        score = masked_head(score, inside)
        m_own = query_rows(stat_ref, 0, rows, group)
        m = jnp.maximum(m_own, jnp.max(score, axis=0, keepdims=True))
        e = jnp.exp2(score - m)
        keep = jnp.exp2(m_own - m)
        total = query_rows(stat_ref, group, rows, group) * keep + jnp.sum(e, axis=0, keepdims=True)
        moment = query_rows(stat_ref, 2 * group, rows, group) * keep + jnp.sum(e * dprob, axis=0, keepdims=True)
        inv = 1.0 / total
        delta = moment * inv
        lse = m + jnp.log2(total)
        for g in range(group):
            spot = slice(g * BLOCK, (g + 1) * BLOCK)
            fin_ref[0, g : g + 1, rows] = lse[:, spot]
            fin_ref[0, group + g : group + g + 1, rows] = delta[:, spot]
        p = e * inv
        return p.astype(BF16), (p * (dprob - delta)).astype(BF16)

    def grads(i, pb, ds):
        rows, low = slice(i * BLOCK, (i + 1) * BLOCK), i * BLOCK
        dq = dot(ds, kh[low:], TN)
        for g in range(group):
            dq_ref[rows, g * dim : (g + 1) * dim] = dq[g * BLOCK : (g + 1) * BLOCK]
        add_up(dka_ref, low, dot(ds, heads(qh_ref, rows, group), NN), 0)
        add_up(dva_ref, low, dot(pb, heads(g_ref, rows, group), NN), 0)

    run_units(reversed(range(tok // BLOCK)), products, soft, grads)
    part = jnp.zeros((8, dim), F32)
    for j in range(tok // BLOCK):
        rows = slice(j * BLOCK, (j + 1) * BLOCK)
        dy = unturn(dka_ref[rows, :] * LN2, cosv[rows], sinv[rows])
        x = k_ref[rows, :].astype(F32)
        part = part + jnp.sum((dy * x * inverse_rms(x)).reshape(BLOCK // 8, 8, dim), axis=0)
        back_ref[rows, :dim] = dy.astype(BF16)
        back_ref[rows, dim:] = dva_ref[rows, :].astype(BF16)
    part_ref[0] = part


def run_units(units, products, soft, grads):
    waiting = None
    for unit in units:
        made = products(unit)
        if waiting is not None:
            grads(*waiting)
        waiting = (unit, *soft(unit, *made))
    grads(*waiting)


def own_kernel(
    qh_ref, kh_ref, v_ref, g_ref, q_ref, k_ref, seg_ref, qgain_ref, cos_ref, sin_ref, cdev_ref, sdev_ref,
    fin_ref, dqp_ref, kpart_ref, qg_ref, dy_ref, dv_ref, sums_ref, cosv_ref, sinv_ref, kdoc_ref, qdoc_ref, dka_ref, part_ref,
):
    tok, dim = kh_ref.shape
    group = qh_ref.shape[1] // dim

    @pl.when(pl.program_id(0) == 0)
    def _():
        s = lax.axis_index("seq")
        cosv_ref[...], sinv_ref[...] = turn(cos_ref, sin_ref, cdev_ref, sdev_ref, s + 1)
        onehot = doc_rows(seg_ref[pl.ds(s, 1)][0])
        kdoc_ref[...] = onehot.astype(BF16)
        qdoc_ref[...] = query_side(onehot)
        part_ref[...] = jnp.zeros_like(part_ref)

    cosv, sinv = cosv_ref[...], sinv_ref[...]
    qdoc = qdoc_ref[...]
    kh = kh_ref[...]
    kside = jnp.concatenate([kh, kdoc_ref[...]], axis=1)
    inside = corner(False, group)
    gain = qgain_ref[...]

    def products(i):
        rows, top = slice(i * BLOCK, (i + 1) * BLOCK), (i + 1) * BLOCK
        qside = jnp.concatenate([heads(qh_ref, rows, group), jnp.concatenate([qdoc[rows]] * group, axis=0)], axis=1)
        return dot(kside[:top], qside, NT), dot(v_ref[:top, :], heads(g_ref, rows, group), NT)

    def soft(i, score, dprob):
        rows = slice(i * BLOCK, (i + 1) * BLOCK)
        p = jnp.exp2(masked_tail(score, inside) - query_rows(fin_ref, 0, rows, group))
        ds = p * (dprob - query_rows(fin_ref, group, rows, group))
        return p.astype(BF16), ds.astype(BF16)

    def grads(i, pb, ds):
        rows, top = slice(i * BLOCK, (i + 1) * BLOCK), (i + 1) * BLOCK
        dq_own = dot(ds, kh[:top], TN)
        add_up(dka_ref, 0, dot(ds, heads(qh_ref, rows, group), NN), i)
        add_up(dv_ref, 0, dot(pb, heads(g_ref, rows, group), NN), i)
        for g in range(group):
            cols = slice(g * dim, (g + 1) * dim)
            dq = dqp_ref[rows, cols] + dq_own[g * BLOCK : (g + 1) * BLOCK]
            dy = unturn(dq * SCALE, cosv[rows], sinv[rows])
            x = q_ref[rows, cols].astype(F32)
            rstd = inverse_rms(x)
            part_ref[0] += jnp.sum((dy * x * rstd).reshape(BLOCK // 8, 8, dim), axis=0)
            gy = dy * gain
            mean = jnp.mean(gy * x, axis=-1, keepdims=True)
            qg_ref[rows, cols] = (rstd * gy - x * (rstd * rstd * rstd * mean)).astype(BF16)

    run_units(range(tok // BLOCK), products, soft, grads)
    kpart = kpart_ref[0]
    for j in range(tok // BLOCK):
        rows = slice(j * BLOCK, (j + 1) * BLOCK)
        dy = unturn(dka_ref[rows, :] * LN2, cosv[rows], sinv[rows])
        x = k_ref[rows, :].astype(F32)
        kpart = kpart + jnp.sum((dy * x * inverse_rms(x)).reshape(BLOCK // 8, 8, dim), axis=0)
        dy_ref[rows, :] = dy
    part_ref[1] += kpart
    sums_ref[...] = jnp.concatenate([jnp.sum(part_ref[n], axis=0, keepdims=True) for n in range(2)], axis=0)


def finish_kernel(k_ref, dy_ref, dv_ref, back_ref, kgain_ref, kg_ref, vg_ref):
    dim = k_ref.shape[1]
    x = k_ref[...].astype(F32)
    rstd = inverse_rms(x)
    gy = (dy_ref[...] + back_ref[:, :dim].astype(F32)) * kgain_ref[...]
    mean = jnp.mean(gy * x, axis=-1, keepdims=True)
    kg_ref[...] = (rstd * gy - x * (rstd * rstd * rstd * mean)).astype(BF16)
    vg_ref[...] = (dv_ref[...] + back_ref[:, dim:].astype(F32)).astype(BF16)


def pairwise(x, axis, step):
    return x + lax.ppermute(x, axis, [(i, i ^ step) for i in range(lax.axis_size(axis))])


def local(q_raw, k_raw, values, grad_out, segment_ids, q_gain, k_gain):
    tok = q_raw.shape[0]
    dim = q_gain.shape[0]
    q_local = q_raw.shape[1] // dim
    kv_local = k_raw.shape[1] // dim
    group = q_local // kv_local
    devices = lax.axis_size("seq")
    cos, sin, cdev, sdev = tables(tok, devices, dim)
    seg = segment_ids.reshape(devices, tok // 128, 128)
    qgain, kgain = q_gain.reshape(1, dim), k_gain.reshape(1, dim)

    k_prev = shifted(k_raw, "seq", 1)
    v_prev = shifted(values, "seq", 1)

    def whole(a):
        return pl.BlockSpec(a.shape, lambda h: (0,) * a.ndim)

    qspec = pl.BlockSpec((tok, group * dim), lambda h: (0, h))
    kspec = pl.BlockSpec((tok, dim), lambda h: (0, h))
    pair_spec = pl.BlockSpec((tok, 2 * dim), lambda h: (0, h))
    stat_spec = pl.BlockSpec((1, 8, tok), lambda h: (h, 0, 0))
    stat_shape = jax.ShapeDtypeStruct((kv_local, 8, tok), F32)
    turns = (cos, sin, cdev, sdev)
    turn_specs = [whole(a) for a in turns]
    params = pltpu.CompilerParams(vmem_limit_bytes=60 * 1024 * 1024)
    roomy = pltpu.CompilerParams(vmem_limit_bytes=57 * 1024 * 1024)
    part_spec = pl.BlockSpec((1, 8, dim), lambda h: (h, 0, 0))
    prep = [pltpu.VMEM((tok, dim), F32)] * 2 + [pltpu.VMEM((tok, DOCS), BF16)] * 2
    total = pltpu.VMEM((tok, dim), F32)

    def cost(products):
        pairs = q_local * tok * tok * 5 // 8
        return pl.CostEstimate(
            flops=2 * products * pairs * dim * 2, bytes_accessed=4 << 20, transcendentals=pairs
        )

    qh, kh, stat = pl.pallas_call(
        stats_kernel,
        grid=(kv_local,),
        in_specs=[qspec, kspec, kspec, qspec, whole(seg), whole(qgain), whole(kgain)] + turn_specs,
        out_specs=[qspec, kspec, stat_spec],
        out_shape=[
            jax.ShapeDtypeStruct(q_raw.shape, BF16),
            jax.ShapeDtypeStruct(k_raw.shape, BF16),
            stat_shape,
        ],
        scratch_shapes=prep[:3] + [pltpu.VMEM((dim + DOCS, tok), BF16), pltpu.VMEM((dim, tok), BF16)],
        compiler_params=params,
        cost_estimate=cost(2),
        name="own_statistics",
    )(q_raw, k_raw, values, grad_out, seg, qgain, kgain, *turns)

    dq_prev, back, fin, kpart_prev = pl.pallas_call(
        halo_kernel,
        grid=(kv_local,),
        in_specs=[qspec, kspec, kspec, qspec, whole(seg), whole(kgain)] + turn_specs + [stat_spec],
        out_specs=[qspec, pair_spec, stat_spec, part_spec],
        out_shape=[
            jax.ShapeDtypeStruct(q_raw.shape, F32),
            jax.ShapeDtypeStruct((tok, 2 * kv_local * dim), BF16),
            stat_shape,
            jax.ShapeDtypeStruct((kv_local, 8, dim), F32),
        ],
        scratch_shapes=prep + [total, total],
        compiler_params=roomy,
        cost_estimate=cost(5),
        name="previous_keys",
    )(qh, k_prev, v_prev, grad_out, seg, kgain, *turns, stat)

    back = shifted(back, "seq", -1)

    q_grad, dy_own, dv_own, sums = pl.pallas_call(
        own_kernel,
        grid=(kv_local,),
        in_specs=[qspec, kspec, kspec, qspec, qspec, kspec, whole(seg), whole(qgain)]
        + turn_specs
        + [stat_spec, qspec, part_spec],
        out_specs=[qspec, kspec, kspec, pl.BlockSpec((2, dim), lambda h: (0, 0))],
        out_shape=[
            jax.ShapeDtypeStruct(q_raw.shape, BF16),
            jax.ShapeDtypeStruct(k_raw.shape, F32),
            jax.ShapeDtypeStruct(k_raw.shape, F32),
            jax.ShapeDtypeStruct((2, dim), F32),
        ],
        scratch_shapes=prep + [total, pltpu.VMEM((2, 8, dim), F32)],
        compiler_params=params,
        cost_estimate=cost(5),
        name="own_keys",
    )(qh, kh, values, grad_out, q_raw, k_raw, seg, qgain, *turns, fin, dq_prev, kpart_prev)

    finish = pl.pallas_call(
        finish_kernel,
        grid=(kv_local,),
        in_specs=[kspec] * 3 + [pair_spec, whole(kgain)],
        out_specs=[kspec, kspec],
        out_shape=[jax.ShapeDtypeStruct(k_raw.shape, BF16)] * 2,
        compiler_params=roomy,
        cost_estimate=pl.CostEstimate(flops=1 << 20, bytes_accessed=5 << 20, transcendentals=0),
        name="add_returned",
    )
    for step in (("head", 1), ("head", 2), ("seq", 1)):
        sums = pairwise(sums, *step)
    sums, back = lax.optimization_barrier((sums, back))
    for step in (("seq", 2), ("seq", 4), ("seq", 8), ("seq", 16), ("head", 4)):
        sums = pairwise(sums, *step)
        if step == ("seq", 8):
            sums, (k_grad, v_grad) = lax.optimization_barrier(
                (sums, finish(k_raw, dy_own, dv_own, back, kgain))
            )
    return (q_grad, k_grad, v_grad, sums[0], sums[1])


def solution(mesh):
    in_specs = (
        P("seq", "head"),
        P("seq", "head"),
        P("seq", "head"),
        P("seq", "head"),
        P(),
        P(),
        P(),
    )
    out_specs = (P("seq", "head"), P("seq", "head"), P("seq", "head"), P(), P())
    return jax.shard_map(local, mesh=mesh, in_specs=in_specs, out_specs=out_specs, check_vma=False)
```

time: 96.5 us -> 85.3 us (0.88)
  Pallas kernels: 48.4 us -> 39.6 us
  starting transfers between devices: 29.1 us -> 23.4 us
  waiting for transfers between devices: 15.7 us -> 19.2 us
    pallas_call x1, Pallas kernels: 19 us -> 13.6 us  [local(): pl.pallas_call(halo_kernel, grid=(kv_local,), in_specs=[qspec, kspec, ksp...]
    ppermute x8, starting transfers between devices: 18.9 us -> 15.1 us  [pairwise(): lax.ppermute(x, axis, [(i, i ^ step) for i in range(lax.axis_size(axis))])]
    ppermute x8, waiting for transfers between devices: 15.7 us -> 19.2 us  [pairwise(): lax.ppermute(x, axis, [(i, i ^ step) for i in range(lax.axis_size(axis))])]
    pallas_call x1, Pallas kernels: 14.6 us -> 12.6 us  [local(): pl.pallas_call(own_kernel, grid=(kv_local,), in_specs=[qspec, kspec, kspe...]
    ppermute x4 -> x3, starting transfers between devices: 10.1 us -> 8.21 us  [shifted(): return lax.ppermute(block, axis, route)]
    pallas_call x1, Pallas kernels: 11.7 us -> 10.2 us  [local(): pl.pallas_call(stats_kernel, grid=(kv_local,), in_specs=[qspec, kspec, ks...]
  transfers between devices with their start and end apart: 12 -> 11, of which waited for: 8 -> 7; matrix products, arithmetic and copies ran while one was open for 1% -> 1% of each run, Pallas kernels for 31% -> 31%
where the time goes in v2:
time: 85.3 us; the launch traced here: 85 us
  Pallas kernels  39.6 us (46%)
  starting transfers between devices  23.4 us (27%)
  waiting for transfers between devices  19.2 us (23%)
  local copies, waits for them, and re-layouts  1.47 us (2%)
    ppermute x8, waiting for transfers between devices, pairwise(): lax.ppermute(x, axis, [(i, i ^ step) for i in range(lax.axis_size(axis))])  19.2 us
    ppermute x8, starting transfers between devices, pairwise(): lax.ppermute(x, axis, [(i, i ^ step) for i in range(lax.axis_size(axis))])  15.1 us
    pallas_call x1, Pallas kernels, local(): pl.pallas_call(halo_kernel, grid=(kv_local,), in_specs=[qspec, kspec, ksp...  13.6 us
    pallas_call x1, Pallas kernels, local(): pl.pallas_call(own_kernel, grid=(kv_local,), in_specs=[qspec, kspec, kspe...  12.6 us
    pallas_call x1, Pallas kernels, local(): pl.pallas_call(stats_kernel, grid=(kv_local,), in_specs=[qspec, kspec, ks...  10.2 us
    ppermute x3, starting transfers between devices, shifted(): return lax.ppermute(block, axis, route)  8.21 us
    pallas_call x1, Pallas kernels, local(): finish(k_raw, dy_own, dv_own, back, kgain)  3.17 us
  transfers between devices with their start and end apart: 11, of which 7 were waited for; matrix products, arithmetic and copies ran while one was open for 1% of the time, Pallas kernels for 31%

profile of v2, /device:TPU:14, one launch (start us, length us, event | category | flops | bytes accessed | tf_op | source)
XLA Modules:
  0.0 85.0 jit_solution(5943152965667589703)
XLA Ops:
  0.6 1.9 %collective-permute-start.1 = (bf16[1024,256]{1,0:T(8,128)(2,1)}, bf16[1024,256]{1,0:T(8,128)(2,1)S(1)}, u32[]{:S(2)}, u32[]{:S(2)}) collective-permute-start(bf16[1024,256]{1,0:T(8,128)(2,1)} %v_ref.3), channel_id=1, source_target_pairs={{0,8},{8,16},{16,24},{24,32},{32,40},{40,48},{48,56},{56,64},{64,7... | collective-permute-start | bytes 1572872 | tf_op jit(solution)/shard_map/ppermute | solution.py:31
  2.6 4.2 %collective-permute-start = (bf16[1024,256]{1,0:T(8,128)(2,1)}, bf16[1024,256]{1,0:T(8,128)(2,1)S(1)}, u32[]{:S(2)}, u32[]{:S(2)}) collective-permute-start(bf16[1024,256]{1,0:T(8,128)(2,1)} %k_ref.5), channel_id=1, source_target_pairs={{0,8},{8,16},{16,24},{24,32},{32,40},{40,48},{48,56},{56,64},{64,7... | collective-permute-start | bytes 1572872 | tf_op jit(solution)/shard_map/ppermute | solution.py:31
  6.8 10.2 %own_statistics.1 = (bf16[1024,512]{1,0:T(8,128)(2,1)}, bf16[1024,256]{1,0:T(8,128)(2,1)}, f32[2,8,1024]{2,1,0:T(8,128)}) custom-call(bf16[1024,512]{1,0:T(8,128)(2,1)} %q_ref.3, bf16[1024,256]{1,0:T(8,128)(2,1)} %k_ref.5, bf16[1024,256]{1,0:T(8,128)(2,1)} %v_ref.3, bf16[1024,512]{1,0:T(8,128)(2,1)} %g_ref.5, s32[32,8,128]{2,1,0:T(8,128)} %bitcast.10, ...), custom_call_target="tpu_custom_call" | custom-call | flops 2684354560 | bytes 4194304 | tf_op jit(solution)/shard_map/own_statistics/pallas_call | solution.py:346
  17.0 0.0 collective-permute-done.1.v_ref
  17.0 0.0 copy-start.1
  17.0 0.0 collective-permute-done.k_ref
  17.0 0.0 copy-start.2
  17.0 0.8 copy-done.1
  17.8 0.2 copy-done.2
  18.0 13.6 %previous_keys.1 = (f32[1024,512]{1,0:T(8,128)}, bf16[1024,512]{1,0:T(8,128)(2,1)}, f32[2,8,1024]{2,1,0:T(8,128)}, f32[2,8,128]{2,1,0:T(8,128)}) custom-call(bf16[1024,512]{1,0:T(8,128)(2,1)} %get-tuple-element.23.qh_ref, bf16[1024,256]{1,0:T(8,128)(2,1)} %copy-done.2, bf16[1024,256]{1,0:T(8,128)(2,1)} %copy-done.1, bf16[1024,512]{1,0:T(8,128)(2,1)} %g_ref.5, ...), custom_call_target="tpu_custom_call" | custom-call | flops 6710886400 | bytes 4194304 | tf_op jit(solution)/shard_map/previous_keys/pallas_call | solution.py:362
  31.6 2.1 %collective-permute-start.5 = (bf16[1024,512]{1,0:T(8,128)(2,1)}, bf16[1024,512]{1,0:T(8,128)(2,1)S(1)}, u32[]{:S(2)}, u32[]{:S(2)}) collective-permute-start(bf16[1024,512]{1,0:T(8,128)(2,1)} %get-tuple-element.31), channel_id=1, source_target_pairs={{8,0},{16,8},{24,16},{32,24},{40,32},{48,40},{56,48},{64,56},{72,6... | collective-permute-start | bytes 3145736 | tf_op jit(solution)/shard_map/ppermute | solution.py:31
  33.7 12.6 %own_keys.1 = (bf16[1024,512]{1,0:T(8,128)(2,1)}, f32[1024,256]{1,0:T(8,128)}, f32[1024,256]{1,0:T(8,128)}, f32[2,128]{1,0:T(2,128)}) custom-call(bf16[1024,512]{1,0:T(8,128)(2,1)} %get-tuple-element.23.qh_ref, bf16[1024,256]{1,0:T(8,128)(2,1)} %get-tuple-element.24.kh_ref, bf16[1024,256]{1,0:T(8,128)(2,1)} %v_ref.3, bf16[1024,512]{1,0:T(8,128)(2,1)} %g_ref.5, ...), custom_call_target="tpu_custom_call" | custom-call | flops 6710886400 | bytes 4194304 | tf_op jit(solution)/shard_map/own_keys/pallas_call | solution.py:381
  46.3 0.5 collective-permute-start.2
  46.8 3.3 %collective-permute-done.2 = f32[2,128]{1,0:T(2,128)S(1)} collective-permute-done((f32[2,128]{1,0:T(2,128)}, f32[2,128]{1,0:T(2,128)S(1)}, u32[]{:S(2)}, u32[]{:S(2)}) %collective-permute-start.2) | collective-permute-done | bytes 1056 | tf_op jit(solution)/shard_map/ppermute | solution.py:307
  50.1 0.7 add.24
  50.8 2.3 %collective-permute-start.3 = (f32[2,128]{1,0:T(2,128)S(1)}, f32[2,128]{1,0:T(2,128)S(1)}, u32[]{:S(2)}, u32[]{:S(2)}) collective-permute-start(f32[2,128]{1,0:T(2,128)S(1)} %add.24), channel_id=1, source_target_pairs={{0,2},{1,3},{2,0},{3,1},{4,6},{5,7},{6,4},{7,5},{8,10},{9,11},{10,... | collective-permute-start | bytes 3080 | tf_op jit(solution)/shard_map/ppermute | solution.py:307
  53.1 2.8 %collective-permute-done.3 = f32[2,128]{1,0:T(2,128)S(1)} collective-permute-done((f32[2,128]{1,0:T(2,128)S(1)}, f32[2,128]{1,0:T(2,128)S(1)}, u32[]{:S(2)}, u32[]{:S(2)}) %collective-permute-start.3) | collective-permute-done | bytes 1056 | tf_op jit(solution)/shard_map/ppermute | solution.py:307
  55.9 0.0 collective-permute-start.4
  55.9 1.1 %collective-permute-done.4 = f32[2,128]{1,0:T(2,128)S(1)} collective-permute-done((f32[2,128]{1,0:T(2,128)S(1)}, f32[2,128]{1,0:T(2,128)S(1)}, u32[]{:S(2)}, u32[]{:S(2)}) %collective-permute-start.4) | collective-permute-done | bytes 1056 | tf_op jit(solution)/shard_map/ppermute | solution.py:307
  57.0 0.0 collective-permute-done.5.back_ref
  57.0 0.0 copy-start
  57.0 0.1 collective-permute-start.6
  57.1 3.6 %collective-permute-done.6 = f32[2,128]{1,0:T(2,128)S(1)} collective-permute-done((f32[2,128]{1,0:T(2,128)S(1)}, f32[2,128]{1,0:T(2,128)S(1)}, u32[]{:S(2)}, u32[]{:S(2)}) %collective-permute-start.6) | collective-permute-done | bytes 1056 | tf_op jit(solution)/shard_map/ppermute | solution.py:307
  60.7 1.9 %collective-permute-start.7 = (f32[2,128]{1,0:T(2,128)S(1)}, f32[2,128]{1,0:T(2,128)S(1)}, u32[]{:S(2)}, u32[]{:S(2)}) collective-permute-start(f32[2,128]{1,0:T(2,128)S(1)} %add.27), channel_id=1, source_target_pairs={{0,32},{8,40},{16,48},{24,56},{32,0},{40,8},{48,16},{56,24},{64,96... | collective-permute-start | bytes 3080 | tf_op jit(solution)/shard_map/ppermute | solution.py:307
  62.6 1.7 %collective-permute-done.7 = f32[2,128]{1,0:T(2,128)S(1)} collective-permute-done((f32[2,128]{1,0:T(2,128)S(1)}, f32[2,128]{1,0:T(2,128)S(1)}, u32[]{:S(2)}, u32[]{:S(2)}) %collective-permute-start.7) | collective-permute-done | bytes 1056 | tf_op jit(solution)/shard_map/ppermute | solution.py:307
  64.3 4.4 %collective-permute-start.8 = (f32[2,128]{1,0:T(2,128)S(1)}, f32[2,128]{1,0:T(2,128)S(1)}, u32[]{:S(2)}, u32[]{:S(2)}) collective-permute-start(f32[2,128]{1,0:T(2,128)S(1)} %add.28), channel_id=1, source_target_pairs={{0,64},{8,72},{16,80},{24,88},{32,96},{40,104},{48,112},{56,120},{... | collective-permute-start | bytes 3080 | tf_op jit(solution)/shard_map/ppermute | solution.py:307
  68.6 0.0 copy-done
  68.7 3.2 %add_returned.1 = (bf16[1024,256]{1,0:T(8,128)(2,1)}, bf16[1024,256]{1,0:T(8,128)(2,1)}) custom-call(bf16[1024,256]{1,0:T(8,128)(2,1)} %k_ref.5, f32[1024,256]{1,0:T(8,128)} %get-tuple-element.33.dy_ref, f32[1024,256]{1,0:T(8,128)} %get-tuple-element.34.dv_ref, bf16[1024,512]{1,0:T(8,128)(2,1)} %copy-done, f32[1,128]{1,0:T(1,128)} %bitcast.9), custom_call_target="tpu_custom_call" | custom-call | flops 1048576 | bytes 5242880 | tf_op jit(solution)/shard_map/add_returned/pallas_call | solution.py:417
  71.8 0.0 collective-permute-done.8
  71.8 4.8 %collective-permute-start.9 = (f32[2,128]{1,0:T(2,128)S(1)}, f32[2,128]{1,0:T(2,128)S(1)}, u32[]{:S(2)}, u32[]{:S(2)}) collective-permute-start(f32[2,128]{1,0:T(2,128)S(1)} %add.29), channel_id=1, source_target_pairs={{0,128},{8,136},{16,144},{24,152},{32,160},{40,168},{48,176},{56,1... | collective-permute-start | bytes 3080 | tf_op jit(solution)/shard_map/ppermute | solution.py:307
  76.7 2.7 %collective-permute-done.9 = f32[2,128]{1,0:T(2,128)S(1)} collective-permute-done((f32[2,128]{1,0:T(2,128)S(1)}, f32[2,128]{1,0:T(2,128)S(1)}, u32[]{:S(2)}, u32[]{:S(2)}) %collective-permute-start.9) | collective-permute-done | bytes 1056 | tf_op jit(solution)/shard_map/ppermute | solution.py:307
  79.4 1.1 %collective-permute-start.10 = (f32[2,128]{1,0:T(2,128)S(1)}, f32[2,128]{1,0:T(2,128)S(1)}, u32[]{:S(2)}, u32[]{:S(2)}) collective-permute-start(f32[2,128]{1,0:T(2,128)S(1)} %add.30), channel_id=1, source_target_pairs={{0,4},{1,5},{2,6},{3,7},{4,0},{5,1},{6,2},{7,3},{8,12},{9,13},{10,... | collective-permute-start | bytes 3080 | tf_op jit(solution)/shard_map/ppermute | solution.py:307
  80.5 4.0 %collective-permute-done.10 = f32[2,128]{1,0:T(2,128)S(1)} collective-permute-done((f32[2,128]{1,0:T(2,128)S(1)}, f32[2,128]{1,0:T(2,128)S(1)}, u32[]{:S(2)}, u32[]{:S(2)}) %collective-permute-start.10) | collective-permute-done | bytes 1056 | tf_op jit(solution)/shard_map/ppermute | solution.py:307
  84.5 0.5 slice_bitcast_fusion
  (7 shorter events, 0.0 us)
Async XLA Ops:
  0.6 16.4 %collective-permute-start.1 = (bf16[1024,256]{1,0:T(8,128)(2,1)}, bf16[1024,256]{1,0:T(8,128)(2,1)S(1)}, u32[]{:S(2)}, u32[]{:S(2)}) collective-permute-start(bf16[1024,256]{1,0:T(8,128)(2,1)} %v_ref.3), channel_id=1, source_target_pairs={{0,8},{8,16},{16,24},{24,32},{32,40},{40,48},{48,56},{56,64},{64,7... | collective-permute-start | bytes 1572872 | tf_op jit(solution)/shard_map/ppermute | solution.py:31
  2.6 14.4 %collective-permute-start = (bf16[1024,256]{1,0:T(8,128)(2,1)}, bf16[1024,256]{1,0:T(8,128)(2,1)S(1)}, u32[]{:S(2)}, u32[]{:S(2)}) collective-permute-start(bf16[1024,256]{1,0:T(8,128)(2,1)} %k_ref.5), channel_id=1, source_target_pairs={{0,8},{8,16},{16,24},{24,32},{32,40},{40,48},{48,56},{56,64},{64,7... | collective-permute-start | bytes 1572872 | tf_op jit(solution)/shard_map/ppermute | solution.py:31
  17.0 0.8 copy-start.1
  17.0 0.9 %copy-start.2 = (bf16[1024,256]{1,0:T(8,128)(2,1)}, bf16[1024,256]{1,0:T(8,128)(2,1)S(1)}, u32[]{:S(2)}) copy-start(bf16[1024,256]{1,0:T(8,128)(2,1)S(1)} %collective-permute-done.k_ref) | copy-start | bytes 1572868
  31.6 25.5 %collective-permute-start.5 = (bf16[1024,512]{1,0:T(8,128)(2,1)}, bf16[1024,512]{1,0:T(8,128)(2,1)S(1)}, u32[]{:S(2)}, u32[]{:S(2)}) collective-permute-start(bf16[1024,512]{1,0:T(8,128)(2,1)} %get-tuple-element.31), channel_id=1, source_target_pairs={{8,0},{16,8},{24,16},{32,24},{40,32},{48,40},{56,48},{64,56},{72,6... | collective-permute-start | bytes 3145736 | tf_op jit(solution)/shard_map/ppermute | solution.py:31
  46.3 3.9 %collective-permute-start.2 = (f32[2,128]{1,0:T(2,128)}, f32[2,128]{1,0:T(2,128)S(1)}, u32[]{:S(2)}, u32[]{:S(2)}) collective-permute-start(f32[2,128]{1,0:T(2,128)} %get-tuple-element.30), channel_id=1, source_target_pairs={{0,1},{1,0},{2,3},{3,2},{4,5},{5,4},{6,7},{7,6},{8,9},{9,8},{10,11... | collective-permute-start | bytes 3080 | tf_op jit(solution)/shard_map/ppermute | solution.py:307
  50.8 5.1 %collective-permute-start.3 = (f32[2,128]{1,0:T(2,128)S(1)}, f32[2,128]{1,0:T(2,128)S(1)}, u32[]{:S(2)}, u32[]{:S(2)}) collective-permute-start(f32[2,128]{1,0:T(2,128)S(1)} %add.24), channel_id=1, source_target_pairs={{0,2},{1,3},{2,0},{3,1},{4,6},{5,7},{6,4},{7,5},{8,10},{9,11},{10,... | collective-permute-start | bytes 3080 | tf_op jit(solution)/shard_map/ppermute | solution.py:307
  55.9 1.1 %collective-permute-start.4 = (f32[2,128]{1,0:T(2,128)S(1)}, f32[2,128]{1,0:T(2,128)S(1)}, u32[]{:S(2)}, u32[]{:S(2)}) collective-permute-start(f32[2,128]{1,0:T(2,128)S(1)} %add.25), channel_id=1, source_target_pairs={{0,8},{8,0},{16,24},{24,16},{32,40},{40,32},{48,56},{56,48},{64,72... | collective-permute-start | bytes 3080 | tf_op jit(solution)/shard_map/ppermute | solution.py:307
  57.0 11.6 %copy-start = (bf16[1024,512]{1,0:T(8,128)(2,1)}, bf16[1024,512]{1,0:T(8,128)(2,1)S(1)}, u32[]{:S(2)}) copy-start(bf16[1024,512]{1,0:T(8,128)(2,1)S(1)} %collective-permute-done.5.back_ref) | copy-start | bytes 3145732
  57.0 3.7 %collective-permute-start.6 = (f32[2,128]{1,0:T(2,128)S(1)}, f32[2,128]{1,0:T(2,128)S(1)}, u32[]{:S(2)}, u32[]{:S(2)}) collective-permute-start(f32[2,128]{1,0:T(2,128)S(1)} %add.26), channel_id=1, source_target_pairs={{0,16},{8,24},{16,0},{24,8},{32,48},{40,56},{48,32},{56,40},{64,80... | collective-permute-start | bytes 3080 | tf_op jit(solution)/shard_map/ppermute | solution.py:307
  60.7 3.6 %collective-permute-start.7 = (f32[2,128]{1,0:T(2,128)S(1)}, f32[2,128]{1,0:T(2,128)S(1)}, u32[]{:S(2)}, u32[]{:S(2)}) collective-permute-start(f32[2,128]{1,0:T(2,128)S(1)} %add.27), channel_id=1, source_target_pairs={{0,32},{8,40},{16,48},{24,56},{32,0},{40,8},{48,16},{56,24},{64,96... | collective-permute-start | bytes 3080 | tf_op jit(solution)/shard_map/ppermute | solution.py:307
  64.3 7.5 %collective-permute-start.8 = (f32[2,128]{1,0:T(2,128)S(1)}, f32[2,128]{1,0:T(2,128)S(1)}, u32[]{:S(2)}, u32[]{:S(2)}) collective-permute-start(f32[2,128]{1,0:T(2,128)S(1)} %add.28), channel_id=1, source_target_pairs={{0,64},{8,72},{16,80},{24,88},{32,96},{40,104},{48,112},{56,120},{... | collective-permute-start | bytes 3080 | tf_op jit(solution)/shard_map/ppermute | solution.py:307
  71.8 7.6 %collective-permute-start.9 = (f32[2,128]{1,0:T(2,128)S(1)}, f32[2,128]{1,0:T(2,128)S(1)}, u32[]{:S(2)}, u32[]{:S(2)}) collective-permute-start(f32[2,128]{1,0:T(2,128)S(1)} %add.29), channel_id=1, source_target_pairs={{0,128},{8,136},{16,144},{24,152},{32,160},{40,168},{48,176},{56,1... | collective-permute-start | bytes 3080 | tf_op jit(solution)/shard_map/ppermute | solution.py:307
  79.4 5.1 %collective-permute-start.10 = (f32[2,128]{1,0:T(2,128)S(1)}, f32[2,128]{1,0:T(2,128)S(1)}, u32[]{:S(2)}, u32[]{:S(2)}) collective-permute-start(f32[2,128]{1,0:T(2,128)S(1)} %add.30), channel_id=1, source_target_pairs={{0,4},{1,5},{2,6},{3,7},{4,0},{5,1},{6,2},{7,3},{8,12},{9,13},{10,... | collective-permute-start | bytes 3080 | tf_op jit(solution)/shard_map/ppermute | solution.py:307

commit v3 on v2

--- a/solution.py
+++ b/solution.py
@@ -120,7 +120,7 @@
 
 def stats_kernel(
     q_ref, k_ref, v_ref, g_ref, seg_ref, qgain_ref, kgain_ref, cos_ref, sin_ref, cdev_ref, sdev_ref,
-    qh_ref, kh_ref, stat_ref, cosv_ref, sinv_ref, kdoc_ref, qt_ref, gt_ref,
+    qh_ref, kh_ref, stat_ref, kdoc_ref, qdoc_ref, cosv_ref, sinv_ref, qt_ref, gt_ref,
 ):
     tok, dim = k_ref.shape
     group = q_ref.shape[1] // dim
@@ -131,7 +131,8 @@
         cosv_ref[...], sinv_ref[...] = turn(cos_ref, sin_ref, cdev_ref, sdev_ref, s + 1)
         onehot = doc_rows(seg_ref[pl.ds(s, 1)][0])
         kdoc_ref[...] = onehot.astype(BF16)
-        qt_ref[dim:, :] = query_side(onehot).T
+        qdoc_ref[...] = query_side(onehot)
+        qt_ref[dim:, :] = qdoc_ref[...].T
 
     cosv, sinv = cosv_ref[...], sinv_ref[...]
     kh = normed(k_ref[...], kgain_ref[...], cosv, sinv)
@@ -157,8 +158,8 @@
 
 
 def halo_kernel(
-    qh_ref, k_ref, v_ref, g_ref, seg_ref, kgain_ref, cos_ref, sin_ref, cdev_ref, sdev_ref, stat_ref,
-    dq_ref, back_ref, fin_ref, part_ref, cosv_ref, sinv_ref, kdoc_ref, qdoc_ref, dka_ref, dva_ref,
+    qh_ref, k_ref, v_ref, g_ref, seg_ref, qdoc_ref, kgain_ref, cos_ref, sin_ref, cdev_ref, sdev_ref, stat_ref,
+    dq_ref, back_ref, fin_ref, part_ref, cosv_ref, sinv_ref, kdoc_ref, dka_ref, dva_ref,
 ):
     tok, dim = k_ref.shape
     group = qh_ref.shape[1] // dim
@@ -167,7 +168,6 @@
     def _():
         s = lax.axis_index("seq")
         cosv_ref[...], sinv_ref[...] = turn(cos_ref, sin_ref, cdev_ref, sdev_ref, s)
-        qdoc_ref[...] = query_side(doc_rows(seg_ref[pl.ds(s, 1)][0]))
         before = doc_rows(seg_ref[pl.ds(jnp.maximum(s - 1, 0), 1)][0])
         kdoc_ref[...] = jnp.where(s == 0, 1.0, before).astype(BF16)
 
@@ -232,8 +232,8 @@
 
 
 def own_kernel(
-    qh_ref, kh_ref, v_ref, g_ref, q_ref, k_ref, seg_ref, qgain_ref, cos_ref, sin_ref, cdev_ref, sdev_ref,
-    fin_ref, dqp_ref, kpart_ref, qg_ref, dy_ref, dv_ref, sums_ref, cosv_ref, sinv_ref, kdoc_ref, qdoc_ref, dka_ref, part_ref,
+    qh_ref, kh_ref, v_ref, g_ref, q_ref, k_ref, kdoc_ref, qdoc_ref, qgain_ref, cos_ref, sin_ref, cdev_ref, sdev_ref,
+    fin_ref, dqp_ref, kpart_ref, qg_ref, dy_ref, dv_ref, sums_ref, cosv_ref, sinv_ref, dka_ref, part_ref,
 ):
     tok, dim = kh_ref.shape
     group = qh_ref.shape[1] // dim
@@ -242,9 +242,6 @@
     def _():
         s = lax.axis_index("seq")
         cosv_ref[...], sinv_ref[...] = turn(cos_ref, sin_ref, cdev_ref, sdev_ref, s + 1)
-        onehot = doc_rows(seg_ref[pl.ds(s, 1)][0])
-        kdoc_ref[...] = onehot.astype(BF16)
-        qdoc_ref[...] = query_side(onehot)
         part_ref[...] = jnp.zeros_like(part_ref)
 
     cosv, sinv = cosv_ref[...], sinv_ref[...]
@@ -326,6 +323,7 @@
 
     qspec = pl.BlockSpec((tok, group * dim), lambda h: (0, h))
     kspec = pl.BlockSpec((tok, dim), lambda h: (0, h))
+    doc_spec = pl.BlockSpec((tok, DOCS), lambda h: (0, 0))
     pair_spec = pl.BlockSpec((tok, 2 * dim), lambda h: (0, h))
     stat_spec = pl.BlockSpec((1, 8, tok), lambda h: (h, 0, 0))
     stat_shape = jax.ShapeDtypeStruct((kv_local, 8, tok), F32)
@@ -343,17 +341,19 @@
             flops=2 * products * pairs * dim * 2, bytes_accessed=4 << 20, transcendentals=pairs
         )
 
-    qh, kh, stat = pl.pallas_call(
+    qh, kh, stat, kdoc, qdoc = pl.pallas_call(
         stats_kernel,
         grid=(kv_local,),
         in_specs=[qspec, kspec, kspec, qspec, whole(seg), whole(qgain), whole(kgain)] + turn_specs,
-        out_specs=[qspec, kspec, stat_spec],
+        out_specs=[qspec, kspec, stat_spec, doc_spec, doc_spec],
         out_shape=[
             jax.ShapeDtypeStruct(q_raw.shape, BF16),
             jax.ShapeDtypeStruct(k_raw.shape, BF16),
             stat_shape,
+            jax.ShapeDtypeStruct((tok, DOCS), BF16),
+            jax.ShapeDtypeStruct((tok, DOCS), BF16),
         ],
-        scratch_shapes=prep[:3] + [pltpu.VMEM((dim + DOCS, tok), BF16), pltpu.VMEM((dim, tok), BF16)],
+        scratch_shapes=prep[:2] + [pltpu.VMEM((dim + DOCS, tok), BF16), pltpu.VMEM((dim, tok), BF16)],
         compiler_params=params,
         cost_estimate=cost(2),
         name="own_statistics",
@@ -362,7 +362,7 @@
     dq_prev, back, fin, kpart_prev = pl.pallas_call(
         halo_kernel,
         grid=(kv_local,),
-        in_specs=[qspec, kspec, kspec, qspec, whole(seg), whole(kgain)] + turn_specs + [stat_spec],
+        in_specs=[qspec, kspec, kspec, qspec, whole(seg), doc_spec, whole(kgain)] + turn_specs + [stat_spec],
         out_specs=[qspec, pair_spec, stat_spec, part_spec],
         out_shape=[
             jax.ShapeDtypeStruct(q_raw.shape, F32),
@@ -370,18 +370,18 @@
             stat_shape,
             jax.ShapeDtypeStruct((kv_local, 8, dim), F32),
         ],
-        scratch_shapes=prep + [total, total],
+        scratch_shapes=prep[:3] + [total, total],
         compiler_params=roomy,
         cost_estimate=cost(5),
         name="previous_keys",
-    )(qh, k_prev, v_prev, grad_out, seg, kgain, *turns, stat)
+    )(qh, k_prev, v_prev, grad_out, seg, qdoc, kgain, *turns, stat)
 
     back = shifted(back, "seq", -1)
 
     q_grad, dy_own, dv_own, sums = pl.pallas_call(
         own_kernel,
         grid=(kv_local,),
-        in_specs=[qspec, kspec, kspec, qspec, qspec, kspec, whole(seg), whole(qgain)]
+        in_specs=[qspec, kspec, kspec, qspec, qspec, kspec, doc_spec, doc_spec, whole(qgain)]
         + turn_specs
         + [stat_spec, qspec, part_spec],
         out_specs=[qspec, kspec, kspec, pl.BlockSpec((2, dim), lambda h: (0, 0))],
@@ -391,11 +391,11 @@
             jax.ShapeDtypeStruct(k_raw.shape, F32),
             jax.ShapeDtypeStruct((2, dim), F32),
         ],
-        scratch_shapes=prep + [total, pltpu.VMEM((2, 8, dim), F32)],
+        scratch_shapes=prep[:2] + [total, pltpu.VMEM((2, 8, dim), F32)],
         compiler_params=params,
         cost_estimate=cost(5),
         name="own_keys",
-    )(qh, kh, values, grad_out, q_raw, k_raw, seg, qgain, *turns, fin, dq_prev, kpart_prev)
+    )(qh, kh, values, grad_out, q_raw, k_raw, kdoc, qdoc, qgain, *turns, fin, dq_prev, kpart_prev)
 
     finish = pl.pallas_call(
         finish_kernel,

time: 85.3 us -> 85.2 us (level)
  transfers between devices with their start and end apart: 11 -> 11, of which waited for: 7 -> 7; matrix products, arithmetic and copies ran while one was open for 1% -> 1% of each run, Pallas kernels for 31% -> 30%
where the time goes in v3:
time: 85.2 us; the launch traced here: 84.9 us
  Pallas kernels  39.5 us (46%)
  starting transfers between devices  23.3 us (27%)
  waiting for transfers between devices  19.2 us (23%)
  local copies, waits for them, and re-layouts  1.47 us (2%)
    ppermute x8, waiting for transfers between devices, pairwise(): lax.ppermute(x, axis, [(i, i ^ step) for i in range(lax.axis_size(axis))])  19.2 us
    ppermute x8, starting transfers between devices, pairwise(): lax.ppermute(x, axis, [(i, i ^ step) for i in range(lax.axis_size(axis))])  15.1 us
    pallas_call x1, Pallas kernels, local(): pl.pallas_call(halo_kernel, grid=(kv_local,), in_specs=[qspec, kspec, ksp...  13.6 us
    pallas_call x1, Pallas kernels, local(): pl.pallas_call(own_kernel, grid=(kv_local,), in_specs=[qspec, kspec, kspe...  12.5 us
    pallas_call x1, Pallas kernels, local(): pl.pallas_call(stats_kernel, grid=(kv_local,), in_specs=[qspec, kspec, ks...  10.3 us
    ppermute x3, starting transfers between devices, shifted(): return lax.ppermute(block, axis, route)  8.22 us
    pallas_call x1, Pallas kernels, local(): finish(k_raw, dy_own, dv_own, back, kgain)  3.17 us
  transfers between devices with their start and end apart: 11, of which 7 were waited for; matrix products, arithmetic and copies ran while one was open for 1% of the time, Pallas kernels for 30%

profile of v3, /device:TPU:14, one launch (start us, length us, event | category | flops | bytes accessed | tf_op | source)
XLA Modules:
  0.0 84.9 jit_solution(10579008121089649064)
XLA Ops:
  0.6 1.9 %collective-permute-start.1 = (bf16[1024,256]{1,0:T(8,128)(2,1)}, bf16[1024,256]{1,0:T(8,128)(2,1)S(1)}, u32[]{:S(2)}, u32[]{:S(2)}) collective-permute-start(bf16[1024,256]{1,0:T(8,128)(2,1)} %v_ref.3), channel_id=1, source_target_pairs={{0,8},{8,16},{16,24},{24,32},{32,40},{40,48},{48,56},{56,64},{64,7... | collective-permute-start | bytes 1572872 | tf_op jit(solution)/shard_map/ppermute | solution.py:31
  2.6 4.2 %collective-permute-start = (bf16[1024,256]{1,0:T(8,128)(2,1)}, bf16[1024,256]{1,0:T(8,128)(2,1)S(1)}, u32[]{:S(2)}, u32[]{:S(2)}) collective-permute-start(bf16[1024,256]{1,0:T(8,128)(2,1)} %k_ref.5), channel_id=1, source_target_pairs={{0,8},{8,16},{16,24},{24,32},{32,40},{40,48},{48,56},{56,64},{64,7... | collective-permute-start | bytes 1572872 | tf_op jit(solution)/shard_map/ppermute | solution.py:31
  6.8 10.3 %own_statistics.1 = (bf16[1024,512]{1,0:T(8,128)(2,1)}, bf16[1024,256]{1,0:T(8,128)(2,1)}, f32[2,8,1024]{2,1,0:T(8,128)}, bf16[1024,32]{1,0:T(8,128)(2,1)}, bf16[1024,32]{1,0:T(8,128)(2,1)}) custom-call(bf16[1024,512]{1,0:T(8,128)(2,1)} %q_ref.3, bf16[1024,256]{1,0:T(8,128)(2,1)} %k_ref.5, bf16[1024,256]{1,0:T(8,128)(2,1)} %v_ref.3, ...), custom_call_target="tpu_custom_call" | custom-call | flops 2684354560 | bytes 4194304 | tf_op jit(solution)/shard_map/own_statistics/pallas_call | solution.py:344
  17.0 0.0 collective-permute-done.1.v_ref
  17.0 0.0 copy-start.1
  17.0 0.0 collective-permute-done.k_ref
  17.0 0.0 copy-start.2
  17.1 0.8 copy-done.1
  17.8 0.2 copy-done.2
  18.0 13.6 %previous_keys.1 = (f32[1024,512]{1,0:T(8,128)}, bf16[1024,512]{1,0:T(8,128)(2,1)}, f32[2,8,1024]{2,1,0:T(8,128)}, f32[2,8,128]{2,1,0:T(8,128)}) custom-call(bf16[1024,512]{1,0:T(8,128)(2,1)} %get-tuple-element.25.qh_ref, bf16[1024,256]{1,0:T(8,128)(2,1)} %copy-done.2, bf16[1024,256]{1,0:T(8,128)(2,1)} %copy-done.1, bf16[1024,512]{1,0:T(8,128)(2,1)} %g_ref.5, ...), custom_call_target="tpu_custom_call" | custom-call | flops 6710886400 | bytes 4194304 | tf_op jit(solution)/shard_map/previous_keys/pallas_call | solution.py:362
  31.6 2.1 %collective-permute-start.5 = (bf16[1024,512]{1,0:T(8,128)(2,1)}, bf16[1024,512]{1,0:T(8,128)(2,1)S(1)}, u32[]{:S(2)}, u32[]{:S(2)}) collective-permute-start(bf16[1024,512]{1,0:T(8,128)(2,1)} %get-tuple-element.35), channel_id=1, source_target_pairs={{8,0},{16,8},{24,16},{32,24},{40,32},{48,40},{56,48},{64,56},{72,6... | collective-permute-start | bytes 3145736 | tf_op jit(solution)/shard_map/ppermute | solution.py:31
  33.7 12.5 %own_keys.1 = (bf16[1024,512]{1,0:T(8,128)(2,1)}, f32[1024,256]{1,0:T(8,128)}, f32[1024,256]{1,0:T(8,128)}, f32[2,128]{1,0:T(2,128)}) custom-call(bf16[1024,512]{1,0:T(8,128)(2,1)} %get-tuple-element.25.qh_ref, bf16[1024,256]{1,0:T(8,128)(2,1)} %get-tuple-element.26.kh_ref, bf16[1024,256]{1,0:T(8,128)(2,1)} %v_ref.3, bf16[1024,512]{1,0:T(8,128)(2,1)} %g_ref.5, ...), custom_call_target="tpu_custom_call" | custom-call | flops 6710886400 | bytes 4194304 | tf_op jit(solution)/shard_map/own_keys/pallas_call | solution.py:381
  46.2 0.5 collective-permute-start.2
  46.7 3.3 %collective-permute-done.2 = f32[2,128]{1,0:T(2,128)S(1)} collective-permute-done((f32[2,128]{1,0:T(2,128)}, f32[2,128]{1,0:T(2,128)S(1)}, u32[]{:S(2)}, u32[]{:S(2)}) %collective-permute-start.2) | collective-permute-done | bytes 1056 | tf_op jit(solution)/shard_map/ppermute | solution.py:304
  50.0 0.7 add.24
  50.7 2.3 %collective-permute-start.3 = (f32[2,128]{1,0:T(2,128)S(1)}, f32[2,128]{1,0:T(2,128)S(1)}, u32[]{:S(2)}, u32[]{:S(2)}) collective-permute-start(f32[2,128]{1,0:T(2,128)S(1)} %add.24), channel_id=1, source_target_pairs={{0,2},{1,3},{2,0},{3,1},{4,6},{5,7},{6,4},{7,5},{8,10},{9,11},{10,... | collective-permute-start | bytes 3080 | tf_op jit(solution)/shard_map/ppermute | solution.py:304
  53.0 2.8 %collective-permute-done.3 = f32[2,128]{1,0:T(2,128)S(1)} collective-permute-done((f32[2,128]{1,0:T(2,128)S(1)}, f32[2,128]{1,0:T(2,128)S(1)}, u32[]{:S(2)}, u32[]{:S(2)}) %collective-permute-start.3) | collective-permute-done | bytes 1056 | tf_op jit(solution)/shard_map/ppermute | solution.py:304
  55.8 0.0 collective-permute-start.4
  55.8 1.1 %collective-permute-done.4 = f32[2,128]{1,0:T(2,128)S(1)} collective-permute-done((f32[2,128]{1,0:T(2,128)S(1)}, f32[2,128]{1,0:T(2,128)S(1)}, u32[]{:S(2)}, u32[]{:S(2)}) %collective-permute-start.4) | collective-permute-done | bytes 1056 | tf_op jit(solution)/shard_map/ppermute | solution.py:304
  56.9 0.0 collective-permute-done.5.back_ref
  56.9 0.0 copy-start
  56.9 0.1 collective-permute-start.6
  57.0 3.6 %collective-permute-done.6 = f32[2,128]{1,0:T(2,128)S(1)} collective-permute-done((f32[2,128]{1,0:T(2,128)S(1)}, f32[2,128]{1,0:T(2,128)S(1)}, u32[]{:S(2)}, u32[]{:S(2)}) %collective-permute-start.6) | collective-permute-done | bytes 1056 | tf_op jit(solution)/shard_map/ppermute | solution.py:304
  60.6 1.9 %collective-permute-start.7 = (f32[2,128]{1,0:T(2,128)S(1)}, f32[2,128]{1,0:T(2,128)S(1)}, u32[]{:S(2)}, u32[]{:S(2)}) collective-permute-start(f32[2,128]{1,0:T(2,128)S(1)} %add.27), channel_id=1, source_target_pairs={{0,32},{8,40},{16,48},{24,56},{32,0},{40,8},{48,16},{56,24},{64,96... | collective-permute-start | bytes 3080 | tf_op jit(solution)/shard_map/ppermute | solution.py:304
  62.5 1.7 %collective-permute-done.7 = f32[2,128]{1,0:T(2,128)S(1)} collective-permute-done((f32[2,128]{1,0:T(2,128)S(1)}, f32[2,128]{1,0:T(2,128)S(1)}, u32[]{:S(2)}, u32[]{:S(2)}) %collective-permute-start.7) | collective-permute-done | bytes 1056 | tf_op jit(solution)/shard_map/ppermute | solution.py:304
  64.2 4.4 %collective-permute-start.8 = (f32[2,128]{1,0:T(2,128)S(1)}, f32[2,128]{1,0:T(2,128)S(1)}, u32[]{:S(2)}, u32[]{:S(2)}) collective-permute-start(f32[2,128]{1,0:T(2,128)S(1)} %add.28), channel_id=1, source_target_pairs={{0,64},{8,72},{16,80},{24,88},{32,96},{40,104},{48,112},{56,120},{... | collective-permute-start | bytes 3080 | tf_op jit(solution)/shard_map/ppermute | solution.py:304
  68.6 0.0 copy-done
  68.6 3.2 %add_returned.1 = (bf16[1024,256]{1,0:T(8,128)(2,1)}, bf16[1024,256]{1,0:T(8,128)(2,1)}) custom-call(bf16[1024,256]{1,0:T(8,128)(2,1)} %k_ref.5, f32[1024,256]{1,0:T(8,128)} %get-tuple-element.37.dy_ref, f32[1024,256]{1,0:T(8,128)} %get-tuple-element.38.dv_ref, bf16[1024,512]{1,0:T(8,128)(2,1)} %copy-done, f32[1,128]{1,0:T(1,128)} %bitcast.9), custom_call_target="tpu_custom_call" | custom-call | flops 1048576 | bytes 5242880 | tf_op jit(solution)/shard_map/add_returned/pallas_call | solution.py:417
  71.7 0.0 collective-permute-done.8
  71.7 4.8 %collective-permute-start.9 = (f32[2,128]{1,0:T(2,128)S(1)}, f32[2,128]{1,0:T(2,128)S(1)}, u32[]{:S(2)}, u32[]{:S(2)}) collective-permute-start(f32[2,128]{1,0:T(2,128)S(1)} %add.29), channel_id=1, source_target_pairs={{0,128},{8,136},{16,144},{24,152},{32,160},{40,168},{48,176},{56,1... | collective-permute-start | bytes 3080 | tf_op jit(solution)/shard_map/ppermute | solution.py:304
  76.5 2.8 %collective-permute-done.9 = f32[2,128]{1,0:T(2,128)S(1)} collective-permute-done((f32[2,128]{1,0:T(2,128)S(1)}, f32[2,128]{1,0:T(2,128)S(1)}, u32[]{:S(2)}, u32[]{:S(2)}) %collective-permute-start.9) | collective-permute-done | bytes 1056 | tf_op jit(solution)/shard_map/ppermute | solution.py:304
  79.3 1.1 %collective-permute-start.10 = (f32[2,128]{1,0:T(2,128)S(1)}, f32[2,128]{1,0:T(2,128)S(1)}, u32[]{:S(2)}, u32[]{:S(2)}) collective-permute-start(f32[2,128]{1,0:T(2,128)S(1)} %add.30), channel_id=1, source_target_pairs={{0,4},{1,5},{2,6},{3,7},{4,0},{5,1},{6,2},{7,3},{8,12},{9,13},{10,... | collective-permute-start | bytes 3080 | tf_op jit(solution)/shard_map/ppermute | solution.py:304
  80.4 4.0 %collective-permute-done.10 = f32[2,128]{1,0:T(2,128)S(1)} collective-permute-done((f32[2,128]{1,0:T(2,128)S(1)}, f32[2,128]{1,0:T(2,128)S(1)}, u32[]{:S(2)}, u32[]{:S(2)}) %collective-permute-start.10) | collective-permute-done | bytes 1056 | tf_op jit(solution)/shard_map/ppermute | solution.py:304
  84.4 0.5 slice_bitcast_fusion
  (7 shorter events, 0.0 us)
Async XLA Ops:
  0.6 16.4 %collective-permute-start.1 = (bf16[1024,256]{1,0:T(8,128)(2,1)}, bf16[1024,256]{1,0:T(8,128)(2,1)S(1)}, u32[]{:S(2)}, u32[]{:S(2)}) collective-permute-start(bf16[1024,256]{1,0:T(8,128)(2,1)} %v_ref.3), channel_id=1, source_target_pairs={{0,8},{8,16},{16,24},{24,32},{32,40},{40,48},{48,56},{56,64},{64,7... | collective-permute-start | bytes 1572872 | tf_op jit(solution)/shard_map/ppermute | solution.py:31
  2.6 14.5 %collective-permute-start = (bf16[1024,256]{1,0:T(8,128)(2,1)}, bf16[1024,256]{1,0:T(8,128)(2,1)S(1)}, u32[]{:S(2)}, u32[]{:S(2)}) collective-permute-start(bf16[1024,256]{1,0:T(8,128)(2,1)} %k_ref.5), channel_id=1, source_target_pairs={{0,8},{8,16},{16,24},{24,32},{32,40},{40,48},{48,56},{56,64},{64,7... | collective-permute-start | bytes 1572872 | tf_op jit(solution)/shard_map/ppermute | solution.py:31
  17.0 0.8 copy-start.1
  17.0 0.9 %copy-start.2 = (bf16[1024,256]{1,0:T(8,128)(2,1)}, bf16[1024,256]{1,0:T(8,128)(2,1)S(1)}, u32[]{:S(2)}) copy-start(bf16[1024,256]{1,0:T(8,128)(2,1)S(1)} %collective-permute-done.k_ref) | copy-start | bytes 1572868
  31.6 25.3 %collective-permute-start.5 = (bf16[1024,512]{1,0:T(8,128)(2,1)}, bf16[1024,512]{1,0:T(8,128)(2,1)S(1)}, u32[]{:S(2)}, u32[]{:S(2)}) collective-permute-start(bf16[1024,512]{1,0:T(8,128)(2,1)} %get-tuple-element.35), channel_id=1, source_target_pairs={{8,0},{16,8},{24,16},{32,24},{40,32},{48,40},{56,48},{64,56},{72,6... | collective-permute-start | bytes 3145736 | tf_op jit(solution)/shard_map/ppermute | solution.py:31
  46.2 3.9 %collective-permute-start.2 = (f32[2,128]{1,0:T(2,128)}, f32[2,128]{1,0:T(2,128)S(1)}, u32[]{:S(2)}, u32[]{:S(2)}) collective-permute-start(f32[2,128]{1,0:T(2,128)} %get-tuple-element.34), channel_id=1, source_target_pairs={{0,1},{1,0},{2,3},{3,2},{4,5},{5,4},{6,7},{7,6},{8,9},{9,8},{10,11... | collective-permute-start | bytes 3080 | tf_op jit(solution)/shard_map/ppermute | solution.py:304
  50.7 5.1 %collective-permute-start.3 = (f32[2,128]{1,0:T(2,128)S(1)}, f32[2,128]{1,0:T(2,128)S(1)}, u32[]{:S(2)}, u32[]{:S(2)}) collective-permute-start(f32[2,128]{1,0:T(2,128)S(1)} %add.24), channel_id=1, source_target_pairs={{0,2},{1,3},{2,0},{3,1},{4,6},{5,7},{6,4},{7,5},{8,10},{9,11},{10,... | collective-permute-start | bytes 3080 | tf_op jit(solution)/shard_map/ppermute | solution.py:304
  55.8 1.1 %collective-permute-start.4 = (f32[2,128]{1,0:T(2,128)S(1)}, f32[2,128]{1,0:T(2,128)S(1)}, u32[]{:S(2)}, u32[]{:S(2)}) collective-permute-start(f32[2,128]{1,0:T(2,128)S(1)} %add.25), channel_id=1, source_target_pairs={{0,8},{8,0},{16,24},{24,16},{32,40},{40,32},{48,56},{56,48},{64,72... | collective-permute-start | bytes 3080 | tf_op jit(solution)/shard_map/ppermute | solution.py:304
  56.9 11.6 %copy-start = (bf16[1024,512]{1,0:T(8,128)(2,1)}, bf16[1024,512]{1,0:T(8,128)(2,1)S(1)}, u32[]{:S(2)}) copy-start(bf16[1024,512]{1,0:T(8,128)(2,1)S(1)} %collective-permute-done.5.back_ref) | copy-start | bytes 3145732
  56.9 3.7 %collective-permute-start.6 = (f32[2,128]{1,0:T(2,128)S(1)}, f32[2,128]{1,0:T(2,128)S(1)}, u32[]{:S(2)}, u32[]{:S(2)}) collective-permute-start(f32[2,128]{1,0:T(2,128)S(1)} %add.26), channel_id=1, source_target_pairs={{0,16},{8,24},{16,0},{24,8},{32,48},{40,56},{48,32},{56,40},{64,80... | collective-permute-start | bytes 3080 | tf_op jit(solution)/shard_map/ppermute | solution.py:304
  60.6 3.6 %collective-permute-start.7 = (f32[2,128]{1,0:T(2,128)S(1)}, f32[2,128]{1,0:T(2,128)S(1)}, u32[]{:S(2)}, u32[]{:S(2)}) collective-permute-start(f32[2,128]{1,0:T(2,128)S(1)} %add.27), channel_id=1, source_target_pairs={{0,32},{8,40},{16,48},{24,56},{32,0},{40,8},{48,16},{56,24},{64,96... | collective-permute-start | bytes 3080 | tf_op jit(solution)/shard_map/ppermute | solution.py:304
  64.2 7.5 %collective-permute-start.8 = (f32[2,128]{1,0:T(2,128)S(1)}, f32[2,128]{1,0:T(2,128)S(1)}, u32[]{:S(2)}, u32[]{:S(2)}) collective-permute-start(f32[2,128]{1,0:T(2,128)S(1)} %add.28), channel_id=1, source_target_pairs={{0,64},{8,72},{16,80},{24,88},{32,96},{40,104},{48,112},{56,120},{... | collective-permute-start | bytes 3080 | tf_op jit(solution)/shard_map/ppermute | solution.py:304
  71.7 7.6 %collective-permute-start.9 = (f32[2,128]{1,0:T(2,128)S(1)}, f32[2,128]{1,0:T(2,128)S(1)}, u32[]{:S(2)}, u32[]{:S(2)}) collective-permute-start(f32[2,128]{1,0:T(2,128)S(1)} %add.29), channel_id=1, source_target_pairs={{0,128},{8,136},{16,144},{24,152},{32,160},{40,168},{48,176},{56,1... | collective-permute-start | bytes 3080 | tf_op jit(solution)/shard_map/ppermute | solution.py:304
  79.3 5.1 %collective-permute-start.10 = (f32[2,128]{1,0:T(2,128)S(1)}, f32[2,128]{1,0:T(2,128)S(1)}, u32[]{:S(2)}, u32[]{:S(2)}) collective-permute-start(f32[2,128]{1,0:T(2,128)S(1)} %add.30), channel_id=1, source_target_pairs={{0,4},{1,5},{2,6},{3,7},{4,0},{5,1},{6,2},{7,3},{8,12},{9,13},{10,... | collective-permute-start | bytes 3080 | tf_op jit(solution)/shard_map/ppermute | solution.py:304
